TPU v7x, 128 devices: a whole 4x4x4 slice. The times are simulated.
128 devices in a mesh: inst: 32 (over y_hi, z, x), tp: 4 (over y_lo, core).
Axes of the slice: x: 4, y: 4 (y_hi: 2, y_lo: 2; y = y_hi * 2 + y_lo), z: 4, core: 2. Of those that a mesh axis runs over, the one named last changes fastest.
Arguments:
- gate_param: float32 [3072, 1280], P(('inst', 'tp')), may hold values from -0.15625 to 0.15625
- gate_grad: float32 [3072, 1280], P(('inst', 'tp')), may hold values from -6 to 6
- gate_m: float32 [3072, 1280], P(('inst', 'tp')), may hold values from -4 to 4
- gate_v: float32 [3072, 1280], P(('inst', 'tp')), may hold values from 0.1 to 3
- down_param: float32 [1280, 3072], P(('inst', 'tp')), may hold values from -0.109375 to 0.109375
- down_grad: float32 [1280, 3072], P(('inst', 'tp')), may hold values from -6 to 6
- down_m: float32 [1280, 3072], P(('inst', 'tp')), may hold values from -4 to 4
- down_v: float32 [1280, 3072], P(('inst', 'tp')), may hold values from 0.1 to 3
Outputs:
- gate_param_new: float32 [3072, 1280], P(('inst', 'tp'))
- gate_m_new: float32 [3072, 1280], P(('inst', 'tp'))
- gate_v_new: float32 [3072, 1280], P(('inst', 'tp'))
- down_param_new: float32 [1280, 3072], P(('inst', 'tp'))
- down_m_new: float32 [1280, 3072], P(('inst', 'tp'))
- down_v_new: float32 [1280, 3072], P(('inst', 'tp'))
- gate_quant: bfloat16 [32, 3072, 1280], P('inst', 'tp')
- gate_scale: float32 [32, 24, 10], P('inst', 'tp')
- down_quant: bfloat16 [32, 1280, 3072], P('inst', None, 'tp')
- down_scale: float32 [32, 10, 24], P('inst', None, 'tp')
All inputs are finite; a program needn't handle non-finite values. Where the computation divides by a largest or mean magnitude, that divisor is 1e-20 or more.
Results may differ from a plain program's by a relative error of at most 0.001.
Values may be sent and summed in bfloat16 or wider, within the bound.
No kernel may reach another device: no remote copies, remote signals or barrier semaphores. Data moves between devices by JAX's collectives and lax.ppermute only.
A program may use at most 128 MiB of HBM per device.

v0:
```python
import jax
import jax.numpy as jnp
from jax import lax
from jax.sharding import PartitionSpec as P

BLOCK = 128


beta_one = 0.9
beta_two = 0.999
adam_eps = 1e-08
step_rate = 0.02
decay_rate = 0.1
correct_one = 0.9999734386011124
correct_two = 0.09520785288629038
scale_eps = 1e-06


def adamw_step(param, grad, moment, second):
    moment_new = beta_one * moment + (1.0 - beta_one) * grad
    second_new = beta_two * second + (1.0 - beta_two) * grad * grad
    update = moment_new / correct_one / (jnp.sqrt(second_new / correct_two) + adam_eps)
    param_new = param - step_rate * (update + decay_rate * param)
    return (param_new, moment_new, second_new)


def quantize(weight):
    row_count, col_count = weight.shape
    blocks = weight.reshape(row_count // BLOCK, BLOCK, col_count // BLOCK, BLOCK)
    block_max = jnp.max(jnp.abs(blocks), axis=(1, 3)) + scale_eps
    coded = (
        (blocks / block_max[:, None, :, None]).reshape(row_count, col_count).astype(jnp.bfloat16)
    )
    return (coded, block_max)


def gate_plain_move(rows_piece, tp_rank, tp_count):
    whole = lax.all_gather(rows_piece, ("inst", "tp"), axis=0, tiled=True)
    share = whole.shape[0] // tp_count
    return lax.dynamic_slice_in_dim(whole, tp_rank * share, share, 0)


def down_plain_move(rows_piece, tp_rank, tp_count):
    row_count, hidden = rows_piece.shape
    whole = lax.all_gather(rows_piece, ("inst", "tp"), axis=0, tiled=True)
    share = hidden // tp_count
    return lax.dynamic_slice_in_dim(whole, tp_rank * share, share, 1)


def body(gate_param, gate_grad, gate_m, gate_v, down_param, down_grad, down_m, down_v):
    gate_new, gate_m_new, gate_v_new = adamw_step(gate_param, gate_grad, gate_m, gate_v)
    down_new, down_m_new, down_v_new = adamw_step(down_param, down_grad, down_m, down_v)
    tp_count = lax.axis_size("tp")
    tp_rank = lax.axis_index("tp")
    gate_local = gate_plain_move(gate_new, tp_rank, tp_count)
    down_local = down_plain_move(down_new, tp_rank, tp_count)
    gate_quant, gate_scale = quantize(gate_local)
    down_quant, down_scale = quantize(down_local)
    return (
        gate_new,
        gate_m_new,
        gate_v_new,
        down_new,
        down_m_new,
        down_v_new,
        gate_quant[None],
        gate_scale[None],
        down_quant[None],
        down_scale[None],
    )


def solution(mesh):
    return jax.shard_map(
        body,
        mesh=mesh,
        in_specs=(
            P(("inst", "tp"), None),
            P(("inst", "tp"), None),
            P(("inst", "tp"), None),
            P(("inst", "tp"), None),
            P(("inst", "tp"), None),
            P(("inst", "tp"), None),
            P(("inst", "tp"), None),
            P(("inst", "tp"), None),
        ),
        out_specs=(
            P(("inst", "tp"), None),
            P(("inst", "tp"), None),
            P(("inst", "tp"), None),
            P(("inst", "tp"), None),
            P(("inst", "tp"), None),
            P(("inst", "tp"), None),
            P("inst", "tp", None),
            P("inst", "tp", None),
            P("inst", None, "tp"),
            P("inst", None, "tp"),
        ),
        check_vma=False,
    )
```

profile of v0, /device:TPU:0, one launch (start us, length us, event | category | flops | bytes accessed | tf_op | source)
XLA Modules:
  0.0 491.2 jit_solution(3379322588430960020)
XLA Ops:
  7.2 0.0 all-gather.6.cloned.1.call-start
  7.2 2.1 multiply_subtract_fusion
  9.3 0.0 all-gather.6.cloned.1.call-update
  9.4 0.0 all-gather.4.cloned.1.call-start
  9.4 1.9 multiply_subtract_fusion.1
  11.3 0.0 all-gather.4.cloned.1.call-update
  11.3 229.2 %all-gather.6.cloned.1.call-done = f32[128,10,3072]{2,1,0:T(8,128)} async-done(((f32[1,10,3072]{2,1,0:T(8,128)}), f32[128,10,3072]{2,1,0:T(8,128)}) %all-gather.6.cloned.1.call-update) | async-done | bytes 15728656 | tf_op jit(solution)/shard_map/all_gather | solution.py:45
  240.5 19.4 %reshape.53 = f32[1280,3072]{1,0:T(8,128)} reshape(f32[128,10,3072]{2,1,0:T(8,128)} %all-gather.6.cloned.1.call-done) | data formatting | bytes 31457280
  259.8 4.5 dynamic-slice_abs_fusion
  264.3 5.5 %abs.15 = f32[10,128,6,128]{3,2,1,0:T(8,128)} reshape(f32[1280,768]{1,0:T(8,128)} %dynamic-slice_abs_fusion) | data formatting | bytes 7864320 | tf_op jit(solution)/shard_map/abs | solution.py:30
  269.8 3.0 reduce_max.19
  272.8 0.4 div.65
  273.2 4.6 fusion.3
  277.8 176.9 %all-gather.4.cloned.1.call-done = f32[3072,1280]{1,0:T(8,128)} async-done(((f32[24,1280]{1,0:T(8,128)}), f32[3072,1280]{1,0:T(8,128)}) %all-gather.4.cloned.1.call-update) | async-done | bytes 15728656 | tf_op jit(solution)/shard_map/all_gather | solution.py:38
  454.7 4.2 constant_dynamic-slice_fusion
  458.9 5.6 %copy.46 = f32[768,1280]{0,1:T(8,128)} copy(f32[768,1280]{1,0:T(8,128)} %constant_dynamic-slice_fusion) | data formatting | bytes 7864320
  464.5 4.4 abs.12
  468.9 5.4 %abs.13 = f32[6,128,10,128]{1,0,3,2:T(8,128)} reshape(f32[768,1280]{0,1:T(8,128)} %abs.12) | data formatting | bytes 7864320 | tf_op jit(solution)/shard_map/abs | solution.py:30
  474.3 3.0 reduce_max.18
  477.3 0.0 copy-start
  477.3 0.4 div.62
  477.7 1.7 copy-done
  479.4 1.4 fusion.2
  480.8 2.3 copy.39
  483.1 0.7 copy.41
  483.7 0.7 copy.40
  (2 shorter events, 0.0 us)
Async XLA Ops:
  7.2 233.3 %all-gather.6.cloned.1.call-start = ((), (), s32[]{:S(2)}) async-start(), calls=%async_computation.1 | async-start | bytes 25362432 | tf_op jit(solution)/shard_map/all_gather | solution.py:45
  9.4 445.3 %all-gather.4.cloned.1.call-start = ((), (), s32[]{:S(2)}) async-start(), calls=%async_computation | async-start | bytes 15851520 | tf_op jit(solution)/shard_map/all_gather | solution.py:38
  477.3 2.1 copy-start
Sparse Core Ops, SparseCore 0:
  10.3 230.1 all-gather.5
  242.8 211.8 all-gather.3
where the time goes:
time: 492 us; the launch traced here: 491 us
  waiting for transfers between devices  406 us (83%)
  local copies, waits for them, and re-layouts  46.2 us (9%)
  other arithmetic  24.8 us (5%)
  between operations  14.1 us (3%)
    all_gather x1, waiting for transfers between devices, down_plain_move(): whole = lax.all_gather(rows_piece, ('inst', 'tp'), axis=0, tiled=True)  229 us
    all_gather x1, waiting for transfers between devices, gate_plain_move(): whole = lax.all_gather(rows_piece, ('inst', 'tp'), axis=0, tiled=True)  177 us
    unnamed x7, local copies, waits for them, and re-layouts  30.3 us
    abs x2, local copies, waits for them, and re-layouts, quantize(): block_max = jnp.max(jnp.abs(blocks), axis=(1, 3)) + scale_eps  10.9 us
  transfers between devices with their start and end apart: 2, of which 2 were waited for; matrix products, arithmetic and copies ran while one was open for 8% of the time, Pallas kernels for 0%

commit v1 on v0

v1 whole, which is shorter than its diff:
```python
import jax
import jax.numpy as jnp
from jax import lax
from jax.experimental import pallas as pl
from jax.experimental.pallas import tpu as pltpu
from jax.sharding import Mesh, PartitionSpec as P

BLOCK = 128
LANES = 128
AXES = ("yh", "z", "x", "yl", "c")
SIZES = (2, 4, 4, 2, 2)
ROWS = ("yh", "z", "x", "yl", "c")
INST = ("yh", "z", "x")
TP = ("yl", "c")

beta_one = 0.9
beta_two = 0.999
adam_eps = 1e-08
step_rate = 0.02
decay_rate = 0.1
correct_one = 0.9999734386011124
correct_two = 0.09520785288629038
scale_eps = 1e-06

GATE_ROWS = 24
GATE_COLS = 1280
DOWN_ROWS = 10
DOWN_COLS = 3072
SHARE = 768
GATE_BLOCKS = GATE_COLS // BLOCK
DOWN_BLOCKS = SHARE // BLOCK
DOWN_LANE = 64


def index_of(yh, z, x, yl, c):
    return (((yh * 4 + z) * 4 + x) * 2 + yl) * 2 + c


def vmem():
    return pl.BlockSpec(memory_space=pltpu.VMEM)


def anywhere():
    return pl.BlockSpec(memory_space=pl.ANY)


def adamw_step(param, grad, moment, second):
    moment_new = beta_one * moment + (1.0 - beta_one) * grad
    second_new = beta_two * second + (1.0 - beta_two) * grad * grad
    update = moment_new / correct_one / (jnp.sqrt(second_new / correct_two) + adam_eps)
    param_new = param - step_rate * (update + decay_rate * param)
    return (param_new, moment_new, second_new)


def adam_kernel(gp, gg, gm, gv, dp, dg, dm, dv, gpo, gmo, gvo, dpo, dmo, dvo, slots):
    gpo[...], gmo[...], gvo[...] = adamw_step(gp[...], gg[...], gm[...], gv[...])
    down, dmo[...], dvo[...] = adamw_step(dp[...], dg[...], dm[...], dv[...])
    dpo[...] = down
    for rank in range(4):
        for k in range(DOWN_BLOCKS):
            col = rank * SHARE + k * BLOCK
            for half in range(2):
                slots[half * 4 + rank, 8 * k : 8 * k + 8, :] = down[0:8, col : col + BLOCK]
                slots[half * 4 + rank, 48 + 2 * k : 50 + 2 * k, :] = down[8:10, col : col + BLOCK]
        for half in range(2):
            slots[half * 4 + rank, 60:64, :] = jnp.zeros((4, LANES), jnp.float32)


def adam(gate, down):
    gate_shape = jax.ShapeDtypeStruct((GATE_ROWS, GATE_COLS), jnp.float32)
    down_shape = jax.ShapeDtypeStruct((DOWN_ROWS, DOWN_COLS), jnp.float32)
    return pl.pallas_call(
        adam_kernel,
        out_shape=(gate_shape,) * 3
        + (down_shape,) * 3
        + (jax.ShapeDtypeStruct((8, 64, LANES), jnp.float32),),
        in_specs=[vmem()] * 8,
        out_specs=(vmem(),) * 7,
    )(*gate, *down)


def block_maxima(rows, first, row_count, blocks):
    size = jnp.abs(rows)
    below = lax.broadcasted_iota(jnp.int32, (row_count, 1), 0) < first
    out = []
    for part in (jnp.where(below, size, 0.0), jnp.where(below, 0.0, size)):
        top = jnp.max(part, axis=0, keepdims=True)
        tall = jnp.concatenate([top[:, k * BLOCK : (k + 1) * BLOCK] for k in range(blocks)], axis=0)
        out.append(jnp.max(tall, axis=1, keepdims=True))
    return out


def maxima_kernel(g0, g1, slots, gate, down, maxima):
    c_lane = lax.broadcasted_iota(jnp.int32, (1, LANES), 1)
    z, x = lax.axis_index("z"), lax.axis_index("x")
    yh = lax.axis_index("yh")
    own = pl.multiple_of(yh * GATE_ROWS, 8)
    other = pl.multiple_of((1 - yh) * GATE_ROWS, 8)
    gate[pl.ds(own, GATE_ROWS), :] = g0[...]
    gate[pl.ds(other, GATE_ROWS), :] = g1[...]
    for h in range(2):
        for s in range(4):
            at = h * 40 + s * DOWN_ROWS
            for k in range(DOWN_BLOCKS):
                col = slice(k * BLOCK, (k + 1) * BLOCK)
                down[at : at + 8, col] = slots[h * 4 + s, 8 * k : 8 * k + 8, :]
                down[at + 8 : at + 10, col] = slots[h * 4 + s, 48 + 2 * k : 50 + 2 * k, :]
    zl, yl = z % 2, z // 2
    at = x * 96 + yl * 48
    blk = at // BLOCK
    low, high = block_maxima(gate[...], (blk + 1) * BLOCK - at, 48, GATE_BLOCKS)
    lane = blk + 3 * zl
    top = jnp.where(c_lane == lane, low, 0.0) + jnp.where(c_lane == lane + 1, high, 0.0)
    maxima[0:GATE_BLOCKS, :] = top
    maxima[GATE_BLOCKS:16, :] = jnp.zeros((16 - GATE_BLOCKS, LANES), jnp.float32)
    at = z * 160 + x * 40
    blk = at // BLOCK
    for h in range(2):
        low, high = block_maxima(down[h * 40 : h * 40 + 40, :], (blk + 1) * BLOCK - at, 40, DOWN_BLOCKS)
        lane = DOWN_LANE + 5 * h + blk
        maxima[0:DOWN_BLOCKS, :] = (
            maxima[0:DOWN_BLOCKS, :]
            + jnp.where(c_lane == lane, low, 0.0)
            + jnp.where(c_lane == lane + 1, high, 0.0)
        )


def partial_maxima(g0, g1, slots):
    return pl.pallas_call(
        maxima_kernel,
        out_shape=(
            jax.ShapeDtypeStruct((48, GATE_COLS), jnp.float32),
            jax.ShapeDtypeStruct((80, SHARE), jnp.float32),
            jax.ShapeDtypeStruct((16, LANES), jnp.float32),
        ),
        in_specs=[vmem()] * 3,
        out_specs=(vmem(),) * 3,
    )(g0, g1, slots)


def quantize_kernel(g0, g1, g2, g3, d0, d1, d2, d3, maxima, gate_out, down_out, scales, gate, down, sems):
    z, x = lax.axis_index("z"), lax.axis_index("x")
    copies = []
    for s, piece in enumerate((g0, g1, g2, g3)):
        zs = (z + 4 - s) % 4
        at = pl.multiple_of((zs % 2) * 96 + (zs // 2) * 48, 16)
        copies.append(pltpu.make_async_copy(piece, gate.at[pl.ds(at, 48), :], sems.at[s]))
    for s, piece in enumerate((d0, d1, d2, d3)):
        xs = (x + 4 - s) % 4
        for h in range(2):
            at = pl.multiple_of(h * 160 + xs * 40, 8)
            copies.append(
                pltpu.make_async_copy(
                    piece.at[pl.ds(h * 40, 40), :], down.at[pl.ds(at, 40), :], sems.at[4 + 2 * s + h]
                )
            )
    for copy in copies:
        copy.start()
    lane = lax.broadcasted_iota(jnp.int32, (1, LANES), 1)
    top = jnp.max(maxima[...], axis=0) + scale_eps
    scales[...] = top

    def pick(at):
        return jnp.max(jnp.where(lane == at, top, 0.0), axis=1, keepdims=True)

    for copy in copies[:4]:
        copy.wait()
    blk = (x * 96) // BLOCK
    first = (blk + 1) * BLOCK - x * 96
    for zl in range(2):
        low, high = pick(blk + 3 * zl), pick(blk + 3 * zl + 1)
        for j in range(3):
            scale = jnp.where(j * 32 >= first, high, low)
            rows = slice(zl * 96 + j * 32, zl * 96 + j * 32 + 32)
            for k in range(GATE_BLOCKS):
                col = slice(k * BLOCK, (k + 1) * BLOCK)
                gate_out[rows, col] = (gate[rows, col] / scale[k : k + 1, :]).astype(jnp.bfloat16)
    for copy in copies[4:]:
        copy.wait()
    blk = (z * 160) // BLOCK
    first = (blk + 1) * BLOCK - z * 160
    for h in range(2):
        low, high = pick(DOWN_LANE + 5 * h + blk), pick(DOWN_LANE + 5 * h + blk + 1)
        for j in range(5):
            scale = jnp.where(j * 32 >= first, high, low)
            rows = slice(h * 160 + j * 32, h * 160 + j * 32 + 32)
            for k in range(DOWN_BLOCKS):
                col = slice(k * BLOCK, (k + 1) * BLOCK)
                down_out[rows, col] = (down[rows, col] / scale[k : k + 1, :]).astype(jnp.bfloat16)


def quantize(gates, downs, maxima):
    return pl.pallas_call(
        quantize_kernel,
        out_shape=(
            jax.ShapeDtypeStruct((192, GATE_COLS), jnp.bfloat16),
            jax.ShapeDtypeStruct((320, SHARE), jnp.bfloat16),
            jax.ShapeDtypeStruct((16, LANES), jnp.float32),
        ),
        in_specs=[anywhere()] * 8 + [vmem()],
        out_specs=(vmem(),) * 3,
        scratch_shapes=[
            pltpu.VMEM((192, GATE_COLS), jnp.float32),
            pltpu.VMEM((320, SHARE), jnp.float32),
            pltpu.SemaphoreType.DMA((12,)),
        ],
    )(*gates, *downs, maxima)


def place_kernel(g0, g1, g2, g3, d0, d1, d2, d3, gate_out, down_out, sems):
    z, x = lax.axis_index("z"), lax.axis_index("x")
    copies = []
    for s in range(4):
        xs, zs = (x + 4 - s) % 4, (z + 4 - s) % 4
        gate, down = (g0, g1, g2, g3)[s], (d0, d1, d2, d3)[s]
        for h in range(2):
            at = pl.multiple_of(h * 384 + xs * 96, 16)
            copies.append(
                pltpu.make_async_copy(
                    gate.at[pl.ds(h * 96, 96), :], gate_out.at[pl.ds(at, 96), :], sems.at[4 * s + h]
                )
            )
            at = pl.multiple_of(h * 640 + zs * 160, 16)
            copies.append(
                pltpu.make_async_copy(
                    down.at[pl.ds(h * 160, 160), :], down_out.at[pl.ds(at, 160), :], sems.at[4 * s + 2 + h]
                )
            )
    for copy in copies:
        copy.start()
    for copy in copies:
        copy.wait()


def place(gates, downs):
    return pl.pallas_call(
        place_kernel,
        out_shape=(
            jax.ShapeDtypeStruct((SHARE, GATE_COLS), jnp.bfloat16),
            jax.ShapeDtypeStruct((GATE_COLS, SHARE), jnp.bfloat16),
        ),
        in_specs=[vmem()] * 8,
        out_specs=(anywhere(),) * 2,
        scratch_shapes=[pltpu.SemaphoreType.DMA((16,))],
    )(*gates, *downs)


def gate_pairs(flip):
    pairs = []
    for yh in range(2):
        for z in range(4):
            for x in range(4):
                for yl in range(2):
                    for c in range(2):
                        target = index_of(c ^ flip, 2 * yl + z % 2, x, yh, z // 2)
                        pairs.append((index_of(yh, z, x, yl, c), target))
    return pairs


def around(array, axis):
    return [array] + [lax.ppermute(array, axis, [(i, (i + s) % 4) for i in range(4)]) for s in (1, 2, 3)]


def body(gate_param, gate_grad, gate_m, gate_v, down_param, down_grad, down_m, down_v):
    gate_new, gate_m_new, gate_v_new, down_new, down_m_new, down_v_new, slots = adam(
        (gate_param, gate_grad, gate_m, gate_v), (down_param, down_grad, down_m, down_v)
    )
    g0 = lax.ppermute(gate_new, AXES, gate_pairs(0))
    g1 = lax.ppermute(gate_new, AXES, gate_pairs(1))
    slots = lax.all_to_all(slots, ("yh", "yl", "c"), 0, 0, tiled=True)
    gate, down, maxima = partial_maxima(g0, g1, slots)
    gates = around(gate, "z")
    downs = around(down, "x")
    maxima = lax.all_to_all(
        jnp.broadcast_to(maxima[None], (16,) + maxima.shape), ("z", "x"), 0, 0, tiled=True
    )
    gate, down, scales = quantize(gates, downs, maxima)
    gate_quant, down_quant = place(around(gate, "x"), around(down, "z"))
    gate_scale = scales[:GATE_BLOCKS, :6].T
    down_scale = scales[:DOWN_BLOCKS, DOWN_LANE : DOWN_LANE + 10].T
    return (
        gate_new,
        gate_m_new,
        gate_v_new,
        down_new,
        down_m_new,
        down_v_new,
        gate_quant[None],
        gate_scale[None],
        down_quant[None],
        down_scale[None],
    )


def solution(mesh):
    parts = Mesh(mesh.devices.reshape(SIZES), AXES)
    return jax.shard_map(
        body,
        mesh=parts,
        in_specs=(P(ROWS, None),) * 8,
        out_specs=(P(ROWS, None),) * 6
        + (
            P(INST, TP, None),
            P(INST, TP, None),
            P(INST, None, TP),
            P(INST, None, TP),
        ),
        check_vma=False,
    )
```

time: 492 us -> 91 us (0.18)
  the two profiles are of different devices: /device:TPU:0 before, /device:TPU:8 now
where the time goes in v1:
time: 91 us; the launch traced here: 90.5 us
  starting transfers between devices  28.9 us (32%)
  waiting for transfers between devices  26.5 us (29%)
  blocking collectives  15 us (16%)
  Pallas kernels  12.2 us (13%)
  local copies, waits for them, and re-layouts  7.09 us (8%)
    ppermute x12, waiting for transfers between devices, around(): lax.ppermute(array, axis, [(i, (i + s) % 4) for i in range(4)])  22.3 us
    ppermute x12, starting transfers between devices, around(): lax.ppermute(array, axis, [(i, (i + s) % 4) for i in range(4)])  16.4 us
    all_to_all x1, blocking collectives, body(): lax.all_to_all(jnp.broadcast_to(maxima[None], (16,) + maxima.shape), ('z'...  15 us
    unnamed x32, local copies, waits for them, and re-layouts  4.94 us
    all_to_all x1, starting transfers between devices, body(): slots = lax.all_to_all(slots, ('yh', 'yl', 'c'), 0, 0, tiled=True)  4.92 us
    ppermute x1, starting transfers between devices, body(): g1 = lax.ppermute(gate_new, AXES, gate_pairs(1))  4.78 us
    pallas_call x1, Pallas kernels, place(): pl.pallas_call(place_kernel, out_shape=(jax.ShapeDtypeStruct((SHARE, GATE...  4.11 us
    pallas_call x1, Pallas kernels, quantize(): pl.pallas_call(quantize_kernel, out_shape=(jax.ShapeDtypeStruct((192, GAT...  3.61 us
  transfers between devices with their start and end apart: 15, of which 6 were waited for; matrix products, arithmetic and copies ran while one was open for 4% of the time, Pallas kernels for 0%

profile of v1, /device:TPU:8, one launch (start us, length us, event | category | flops | bytes accessed | tf_op | source)
XLA Modules:
  0.0 90.5 jit_solution(17077961977002870744)
XLA Ops:
  0.6 2.5 %shard_map.159 = (f32[24,1280]{1,0:T(8,128)}, f32[24,1280]{1,0:T(8,128)}, f32[24,1280]{1,0:T(8,128)}, f32[10,3072]{1,0:T(8,128)}, f32[10,3072]{1,0:T(8,128)}, /*index=5*/f32[10,3072]{1,0:T(8,128)}, f32[8,64,128]{2,1,0:T(8,128)}) custom-call(f32[24,1280]{1,0:T(8,128)} %gp.1, f32[24,1280]{1,0:T(8,128)} %gg.1, f32[24,1280]{1,0:T(8,128)} %gm.1, f32[24,1280]{1,0:T(8,128)} %gv.1, ...), custom_call_target="tpu_custom_call" | custom-call | tf_op jit(solution)/shard_map/pallas_call | solution.py:72
  3.2 4.9 %all-to-all-start = ((f32[8,64,128]{2,1,0:T(8,128)}), f32[8,64,128]{2,1,0:T(8,128)S(1)}, u32[]{:S(2)}, u32[]{:S(2)}) async-start(f32[8,64,128]{2,1,0:T(8,128)} %get-tuple-element.31), calls=%async_computation | async-start | bytes 524288 | tf_op jit(solution)/shard_map/all_to_all | solution.py:270
  8.1 4.8 %collective-permute-start.1 = (f32[24,1280]{1,0:T(8,128)}, f32[24,1280]{1,0:T(8,128)S(1)}, u32[]{:S(2)}, u32[]{:S(2)}) collective-permute-start(f32[24,1280]{1,0:T(8,128)} %get-tuple-element.40), channel_id=1, source_target_pairs={{0,64},{1,0},{2,96},{3,32},{4,68},{5,4},{6,100},{7,36},{8,72},{9,8... | collective-permute-start | bytes 368648 | tf_op jit(solution)/shard_map/ppermute | solution.py:269
  12.9 2.8 %collective-permute-start = (f32[24,1280]{1,0:T(8,128)}, f32[24,1280]{1,0:T(8,128)S(1)}, u32[]{:S(2)}, u32[]{:S(2)}) collective-permute-start(f32[24,1280]{1,0:T(8,128)} %get-tuple-element.40), channel_id=1, source_target_pairs={{0,0},{1,64},{2,32},{3,96},{4,4},{5,68},{6,36},{7,100},{8,8},{9,72... | collective-permute-start | bytes 368648 | tf_op jit(solution)/shard_map/ppermute | solution.py:268
  15.7 1.7 %collective-permute-done.1.g1 = f32[24,1280]{1,0:T(8,128)S(1)} collective-permute-done((f32[24,1280]{1,0:T(8,128)}, f32[24,1280]{1,0:T(8,128)S(1)}, u32[]{:S(2)}, u32[]{:S(2)}) %collective-permute-start.1) | collective-permute-done | bytes 122912 | tf_op jit(solution)/shard_map/ppermute | solution.py:269
  17.4 2.4 %collective-permute-done.g0 = f32[24,1280]{1,0:T(8,128)S(1)} collective-permute-done((f32[24,1280]{1,0:T(8,128)}, f32[24,1280]{1,0:T(8,128)S(1)}, u32[]{:S(2)}, u32[]{:S(2)}) %collective-permute-start) | collective-permute-done | bytes 122912 | tf_op jit(solution)/shard_map/ppermute | solution.py:268
  19.9 0.6 copy-done.14
  20.5 0.7 copy-done
  21.2 1.9 %shard_map.160 = (f32[48,1280]{1,0:T(8,128)}, f32[80,768]{1,0:T(8,128)}, f32[16,128]{1,0:T(8,128)}) custom-call(f32[24,1280]{1,0:T(8,128)} %copy-done.14, f32[24,1280]{1,0:T(8,128)} %copy-done.13, f32[8,64,128]{2,1,0:T(8,128)} %copy-done), custom_call_target="tpu_custom_call" | custom-call | tf_op jit(solution)/shard_map/pallas_call | solution.py:129
  23.2 4.4 %collective-permute-start.4 = (f32[48,1280]{1,0:T(8,128)}, f32[48,1280]{1,0:T(8,128)S(1)}, u32[]{:S(2)}, u32[]{:S(2)}) collective-permute-start(f32[48,1280]{1,0:T(8,128)} %get-tuple-element.32.g0), channel_id=1, source_target_pairs={{0,48},{16,0},{32,16},{48,32},{1,49},{17,1},{33,17},{49,33},{2,50}... | collective-permute-start | bytes 737288 | tf_op jit(solution)/shard_map/ppermute | solution.py:261
  27.6 1.3 %collective-permute-start.2 = (f32[48,1280]{1,0:T(8,128)}, f32[48,1280]{1,0:T(8,128)S(1)}, u32[]{:S(2)}, u32[]{:S(2)}) collective-permute-start(f32[48,1280]{1,0:T(8,128)} %get-tuple-element.32.g0), channel_id=1, source_target_pairs={{0,16},{16,32},{32,48},{48,0},{1,17},{17,33},{33,49},{49,1},{2,18}... | collective-permute-start | bytes 737288 | tf_op jit(solution)/shard_map/ppermute | solution.py:261
  28.9 2.8 %collective-permute-start.7 = (f32[80,768]{1,0:T(8,128)}, f32[80,768]{1,0:T(8,128)S(1)}, u32[]{:S(2)}, u32[]{:S(2)}) collective-permute-start(f32[80,768]{1,0:T(8,128)} %get-tuple-element.33.d0), channel_id=1, source_target_pairs={{0,12},{4,0},{8,4},{12,8},{1,13},{5,1},{9,5},{13,9},{2,14},{6,2},{... | collective-permute-start | bytes 737288 | tf_op jit(solution)/shard_map/ppermute | solution.py:261
  31.6 0.8 collective-permute-start.6
  32.4 4.5 %collective-permute-done.4.g3 = f32[48,1280]{1,0:T(8,128)S(1)} collective-permute-done((f32[48,1280]{1,0:T(8,128)}, f32[48,1280]{1,0:T(8,128)S(1)}, u32[]{:S(2)}, u32[]{:S(2)}) %collective-permute-start.4) | collective-permute-done | bytes 245792 | tf_op jit(solution)/shard_map/ppermute | solution.py:261
  36.9 1.5 %collective-permute-start.5 = (f32[80,768]{1,0:T(8,128)}, f32[80,768]{1,0:T(8,128)S(1)}, u32[]{:S(2)}, u32[]{:S(2)}) collective-permute-start(f32[80,768]{1,0:T(8,128)} %get-tuple-element.33.d0), channel_id=1, source_target_pairs={{0,4},{4,8},{8,12},{12,0},{1,5},{5,9},{9,13},{13,1},{2,6},{6,10},{... | collective-permute-start | bytes 737288 | tf_op jit(solution)/shard_map/ppermute | solution.py:261
  38.4 0.7 broadcast_in_dim.18
  39.1 15.0 %all_to_all.10.maxima = f32[16,16,128]{2,1,0:T(8,128)} all-to-all(f32[16,16,128]{2,1,0:T(8,128)S(1)} %broadcast_in_dim.18), channel_id=1, replica_groups=mesh['yh'=2,'z'=4,'x'=4,'yl'=2,'c'=2] {'z','x'}, dimensions={0} | all-to-all | bytes 262144 | tf_op jit(solution)/shard_map/all_to_all | solution.py:274
  54.2 0.6 copy-done.8
  55.1 0.7 copy-done.12
  55.8 3.6 %shard_map.161 = (bf16[192,1280]{1,0:T(8,128)(2,1)}, bf16[320,768]{1,0:T(8,128)(2,1)}, f32[16,128]{1,0:T(8,128)}) custom-call(f32[48,1280]{1,0:T(8,128)} %get-tuple-element.32.g0, f32[48,1280]{1,0:T(8,128)} %copy-done.9, f32[48,1280]{1,0:T(8,128)} %copy-done.8, f32[48,1280]{1,0:T(8,128)} %copy-done.7, f32[80,768]{1,0:T(8,128)} %get-tuple-element.33.d0, ...), custom_call_target="tpu_custom_call" | custom-call | tf_op jit(solution)/shard_map/pallas_call | solution.py:193
  59.4 1.0 %collective-permute-start.10 = (bf16[192,1280]{1,0:T(8,128)(2,1)}, bf16[192,1280]{1,0:T(8,128)(2,1)S(1)}, u32[]{:S(2)}, u32[]{:S(2)}) collective-permute-start(bf16[192,1280]{1,0:T(8,128)(2,1)} %get-tuple-element.35.g0), channel_id=1, source_target_pairs={{0,12},{4,0},{8,4},{12,8},{1,13},{5,1},{9,5},{13,9},{2,14},{6,2},{... | collective-permute-start | bytes 1474568 | tf_op jit(solution)/shard_map/ppermute | solution.py:261
  60.4 1.7 %collective-permute-start.9 = (bf16[192,1280]{1,0:T(8,128)(2,1)}, bf16[192,1280]{1,0:T(8,128)(2,1)S(1)}, u32[]{:S(2)}, u32[]{:S(2)}) collective-permute-start(bf16[192,1280]{1,0:T(8,128)(2,1)} %get-tuple-element.35.g0), channel_id=1, source_target_pairs={{0,8},{4,12},{8,0},{12,4},{1,9},{5,13},{9,1},{13,5},{2,10},{6,14},... | collective-permute-start | bytes 1474568 | tf_op jit(solution)/shard_map/ppermute | solution.py:261
  62.1 1.1 %collective-permute-start.13 = (bf16[320,768]{1,0:T(8,128)(2,1)}, bf16[320,768]{1,0:T(8,128)(2,1)S(1)}, u32[]{:S(2)}, u32[]{:S(2)}) collective-permute-start(bf16[320,768]{1,0:T(8,128)(2,1)} %get-tuple-element.36.d0), channel_id=1, source_target_pairs={{0,48},{16,0},{32,16},{48,32},{1,49},{17,1},{33,17},{49,33},{2,50}... | collective-permute-start | bytes 1474568 | tf_op jit(solution)/shard_map/ppermute | solution.py:261
  63.2 1.5 %collective-permute-start.12 = (bf16[320,768]{1,0:T(8,128)(2,1)}, bf16[320,768]{1,0:T(8,128)(2,1)S(1)}, u32[]{:S(2)}, u32[]{:S(2)}) collective-permute-start(bf16[320,768]{1,0:T(8,128)(2,1)} %get-tuple-element.36.d0), channel_id=1, source_target_pairs={{0,32},{16,48},{32,0},{48,16},{1,33},{17,49},{33,1},{49,17},{2,34}... | collective-permute-start | bytes 1474568 | tf_op jit(solution)/shard_map/ppermute | solution.py:261
  64.7 9.1 %collective-permute-done.10.g3 = bf16[192,1280]{1,0:T(8,128)(2,1)S(1)} collective-permute-done((bf16[192,1280]{1,0:T(8,128)(2,1)}, bf16[192,1280]{1,0:T(8,128)(2,1)S(1)}, u32[]{:S(2)}, u32[]{:S(2)}) %collective-permute-start.10) | collective-permute-done | bytes 491552 | tf_op jit(solution)/shard_map/ppermute | solution.py:261
  74.1 0.7 slice_bitcast_fusion.1
  75.4 0.7 slice_bitcast_fusion
  76.1 0.7 copy.19
  76.8 6.2 %collective-permute-done.8.g1 = bf16[192,1280]{1,0:T(8,128)(2,1)S(1)} collective-permute-done((bf16[192,1280]{1,0:T(8,128)(2,1)}, bf16[192,1280]{1,0:T(8,128)(2,1)S(1)}, u32[]{:S(2)}, u32[]{:S(2)}) %collective-permute-start.8) | collective-permute-done | bytes 491552 | tf_op jit(solution)/shard_map/ppermute | solution.py:261
  83.0 2.5 %collective-permute-done.11.d1 = bf16[320,768]{1,0:T(8,128)(2,1)S(1)} collective-permute-done((bf16[320,768]{1,0:T(8,128)(2,1)}, bf16[320,768]{1,0:T(8,128)(2,1)S(1)}, u32[]{:S(2)}, u32[]{:S(2)}) %collective-permute-start.11) | collective-permute-done | bytes 491552 | tf_op jit(solution)/shard_map/ppermute | solution.py:261
  85.6 0.8 copy-done.6
  86.3 4.1 %shard_map.162 = (bf16[768,1280]{1,0:T(8,128)(2,1)}, bf16[1280,768]{1,0:T(8,128)(2,1)}) custom-call(bf16[192,1280]{1,0:T(8,128)(2,1)} %get-tuple-element.35.g0, bf16[192,1280]{1,0:T(8,128)(2,1)} %copy-done.3, bf16[192,1280]{1,0:T(8,128)(2,1)} %copy-done.2, bf16[192,1280]{1,0:T(8,128)(2,1)} %copy-done.1, bf16[320,768]{1,0:T(8,128)(2,1)} %get-tuple-element.36.d0, ...), custom_call_target="tpu_custom_call" | custom-call | tf_op jit(solution)/shard_map/pallas_call | solution.py:236
  (38 shorter events, 1.2 us)
Async XLA Ops:
  3.2 16.7 %all-to-all-start = ((f32[8,64,128]{2,1,0:T(8,128)}), f32[8,64,128]{2,1,0:T(8,128)S(1)}, u32[]{:S(2)}, u32[]{:S(2)}) async-start(f32[8,64,128]{2,1,0:T(8,128)} %get-tuple-element.31), calls=%async_computation | async-start | bytes 524288 | tf_op jit(solution)/shard_map/all_to_all | solution.py:270
  8.1 9.3 %collective-permute-start.1 = (f32[24,1280]{1,0:T(8,128)}, f32[24,1280]{1,0:T(8,128)S(1)}, u32[]{:S(2)}, u32[]{:S(2)}) collective-permute-start(f32[24,1280]{1,0:T(8,128)} %get-tuple-element.40), channel_id=1, source_target_pairs={{0,64},{1,0},{2,96},{3,32},{4,68},{5,4},{6,100},{7,36},{8,72},{9,8... | collective-permute-start | bytes 368648 | tf_op jit(solution)/shard_map/ppermute | solution.py:269
  12.9 7.0 %collective-permute-start = (f32[24,1280]{1,0:T(8,128)}, f32[24,1280]{1,0:T(8,128)S(1)}, u32[]{:S(2)}, u32[]{:S(2)}) collective-permute-start(f32[24,1280]{1,0:T(8,128)} %get-tuple-element.40), channel_id=1, source_target_pairs={{0,0},{1,64},{2,32},{3,96},{4,4},{5,68},{6,36},{7,100},{8,8},{9,72... | collective-permute-start | bytes 368648 | tf_op jit(solution)/shard_map/ppermute | solution.py:268
  17.4 2.5 %copy-start.13 = (f32[24,1280]{1,0:T(8,128)}, f32[24,1280]{1,0:T(8,128)S(1)}, u32[]{:S(2)}) copy-start(f32[24,1280]{1,0:T(8,128)S(1)} %collective-permute-done.1.g1) | copy-start | bytes 368644
  19.9 0.6 copy-start.14
  20.5 0.7 copy-start
  23.2 13.8 %collective-permute-start.4 = (f32[48,1280]{1,0:T(8,128)}, f32[48,1280]{1,0:T(8,128)S(1)}, u32[]{:S(2)}, u32[]{:S(2)}) collective-permute-start(f32[48,1280]{1,0:T(8,128)} %get-tuple-element.32.g0), channel_id=1, source_target_pairs={{0,48},{16,0},{32,16},{48,32},{1,49},{17,1},{33,17},{49,33},{2,50}... | collective-permute-start | bytes 737288 | tf_op jit(solution)/shard_map/ppermute | solution.py:261
  27.6 26.5 %collective-permute-start.3 = (f32[48,1280]{1,0:T(8,128)}, f32[48,1280]{1,0:T(8,128)S(1)}, u32[]{:S(2)}, u32[]{:S(2)}) collective-permute-start(f32[48,1280]{1,0:T(8,128)} %get-tuple-element.32.g0), channel_id=1, source_target_pairs={{0,32},{16,48},{32,0},{48,16},{1,33},{17,49},{33,1},{49,17},{2,34}... | collective-permute-start | bytes 737288 | tf_op jit(solution)/shard_map/ppermute | solution.py:261
  27.6 26.5 %collective-permute-start.2 = (f32[48,1280]{1,0:T(8,128)}, f32[48,1280]{1,0:T(8,128)S(1)}, u32[]{:S(2)}, u32[]{:S(2)}) collective-permute-start(f32[48,1280]{1,0:T(8,128)} %get-tuple-element.32.g0), channel_id=1, source_target_pairs={{0,16},{16,32},{32,48},{48,0},{1,17},{17,33},{33,49},{49,1},{2,18}... | collective-permute-start | bytes 737288 | tf_op jit(solution)/shard_map/ppermute | solution.py:261
  28.9 25.3 %collective-permute-start.7 = (f32[80,768]{1,0:T(8,128)}, f32[80,768]{1,0:T(8,128)S(1)}, u32[]{:S(2)}, u32[]{:S(2)}) collective-permute-start(f32[80,768]{1,0:T(8,128)} %get-tuple-element.33.d0), channel_id=1, source_target_pairs={{0,12},{4,0},{8,4},{12,8},{1,13},{5,1},{9,5},{13,9},{2,14},{6,2},{... | collective-permute-start | bytes 737288 | tf_op jit(solution)/shard_map/ppermute | solution.py:261
  31.6 22.6 %collective-permute-start.6 = (f32[80,768]{1,0:T(8,128)}, f32[80,768]{1,0:T(8,128)S(1)}, u32[]{:S(2)}, u32[]{:S(2)}) collective-permute-start(f32[80,768]{1,0:T(8,128)} %get-tuple-element.33.d0), channel_id=1, source_target_pairs={{0,8},{4,12},{8,0},{12,4},{1,9},{5,13},{9,1},{13,5},{2,10},{6,14},... | collective-permute-start | bytes 737288 | tf_op jit(solution)/shard_map/ppermute | solution.py:261
  36.9 17.3 %copy-start.7 = (f32[48,1280]{1,0:T(8,128)}, f32[48,1280]{1,0:T(8,128)S(1)}, u32[]{:S(2)}) copy-start(f32[48,1280]{1,0:T(8,128)S(1)} %collective-permute-done.4.g3) | copy-start | bytes 737284
  36.9 17.3 %collective-permute-start.5 = (f32[80,768]{1,0:T(8,128)}, f32[80,768]{1,0:T(8,128)S(1)}, u32[]{:S(2)}, u32[]{:S(2)}) collective-permute-start(f32[80,768]{1,0:T(8,128)} %get-tuple-element.33.d0), channel_id=1, source_target_pairs={{0,4},{4,8},{8,12},{12,0},{1,5},{5,9},{9,13},{13,1},{2,6},{6,10},{... | collective-permute-start | bytes 737288 | tf_op jit(solution)/shard_map/ppermute | solution.py:261
  54.1 0.7 copy-start.8
  54.1 0.8 copy-start.9
  54.2 0.8 copy-start.10
  54.2 0.9 copy-start.11
  55.1 0.7 copy-start.12
  59.4 14.4 %collective-permute-start.10 = (bf16[192,1280]{1,0:T(8,128)(2,1)}, bf16[192,1280]{1,0:T(8,128)(2,1)S(1)}, u32[]{:S(2)}, u32[]{:S(2)}) collective-permute-start(bf16[192,1280]{1,0:T(8,128)(2,1)} %get-tuple-element.35.g0), channel_id=1, source_target_pairs={{0,12},{4,0},{8,4},{12,8},{1,13},{5,1},{9,5},{13,9},{2,14},{6,2},{... | collective-permute-start | bytes 1474568 | tf_op jit(solution)/shard_map/ppermute | solution.py:261
  60.4 16.4 %collective-permute-start.9 = (bf16[192,1280]{1,0:T(8,128)(2,1)}, bf16[192,1280]{1,0:T(8,128)(2,1)S(1)}, u32[]{:S(2)}, u32[]{:S(2)}) collective-permute-start(bf16[192,1280]{1,0:T(8,128)(2,1)} %get-tuple-element.35.g0), channel_id=1, source_target_pairs={{0,8},{4,12},{8,0},{12,4},{1,9},{5,13},{9,1},{13,5},{2,10},{6,14},... | collective-permute-start | bytes 1474568 | tf_op jit(solution)/shard_map/ppermute | solution.py:261
  62.1 20.9 %collective-permute-start.8 = (bf16[192,1280]{1,0:T(8,128)(2,1)}, bf16[192,1280]{1,0:T(8,128)(2,1)S(1)}, u32[]{:S(2)}, u32[]{:S(2)}) collective-permute-start(bf16[192,1280]{1,0:T(8,128)(2,1)} %get-tuple-element.35.g0), channel_id=1, source_target_pairs={{0,4},{4,8},{8,12},{12,0},{1,5},{5,9},{9,13},{13,1},{2,6},{6,10},{... | collective-permute-start | bytes 1474568 | tf_op jit(solution)/shard_map/ppermute | solution.py:261
  62.1 20.9 %collective-permute-start.13 = (bf16[320,768]{1,0:T(8,128)(2,1)}, bf16[320,768]{1,0:T(8,128)(2,1)S(1)}, u32[]{:S(2)}, u32[]{:S(2)}) collective-permute-start(bf16[320,768]{1,0:T(8,128)(2,1)} %get-tuple-element.36.d0), channel_id=1, source_target_pairs={{0,48},{16,0},{32,16},{48,32},{1,49},{17,1},{33,17},{49,33},{2,50}... | collective-permute-start | bytes 1474568 | tf_op jit(solution)/shard_map/ppermute | solution.py:261
  63.2 19.8 %collective-permute-start.12 = (bf16[320,768]{1,0:T(8,128)(2,1)}, bf16[320,768]{1,0:T(8,128)(2,1)S(1)}, u32[]{:S(2)}, u32[]{:S(2)}) collective-permute-start(bf16[320,768]{1,0:T(8,128)(2,1)} %get-tuple-element.36.d0), channel_id=1, source_target_pairs={{0,32},{16,48},{32,0},{48,16},{1,33},{17,49},{33,1},{49,17},{2,34}... | collective-permute-start | bytes 1474568 | tf_op jit(solution)/shard_map/ppermute | solution.py:261
  73.8 11.7 %copy-start.1 = (bf16[192,1280]{1,0:T(8,128)(2,1)}, bf16[192,1280]{1,0:T(8,128)(2,1)S(1)}, u32[]{:S(2)}) copy-start(bf16[192,1280]{1,0:T(8,128)(2,1)S(1)} %collective-permute-done.10.g3) | copy-start | bytes 1474564
  73.8 11.7 %collective-permute-start.11 = (bf16[320,768]{1,0:T(8,128)(2,1)}, bf16[320,768]{1,0:T(8,128)(2,1)S(1)}, u32[]{:S(2)}, u32[]{:S(2)}) collective-permute-start(bf16[320,768]{1,0:T(8,128)(2,1)} %get-tuple-element.36.d0), channel_id=1, source_target_pairs={{0,16},{16,32},{32,48},{48,0},{1,17},{17,33},{33,49},{49,1},{2,18}... | collective-permute-start | bytes 1474568 | tf_op jit(solution)/shard_map/ppermute | solution.py:261
  76.8 8.7 %copy-start.2 = (bf16[192,1280]{1,0:T(8,128)(2,1)}, bf16[192,1280]{1,0:T(8,128)(2,1)S(1)}, u32[]{:S(2)}) copy-start(bf16[192,1280]{1,0:T(8,128)(2,1)S(1)} %collective-permute-done.9.g2) | copy-start | bytes 1474564
  83.0 2.6 %copy-start.3 = (bf16[192,1280]{1,0:T(8,128)(2,1)}, bf16[192,1280]{1,0:T(8,128)(2,1)S(1)}, u32[]{:S(2)}) copy-start(bf16[192,1280]{1,0:T(8,128)(2,1)S(1)} %collective-permute-done.8.g1) | copy-start | bytes 1474564
  83.0 2.6 %copy-start.4 = (bf16[320,768]{1,0:T(8,128)(2,1)}, bf16[320,768]{1,0:T(8,128)(2,1)S(1)}, u32[]{:S(2)}) copy-start(bf16[320,768]{1,0:T(8,128)(2,1)S(1)} %collective-permute-done.13.d3) | copy-start | bytes 1474564
  83.0 2.6 %copy-start.5 = (bf16[320,768]{1,0:T(8,128)(2,1)}, bf16[320,768]{1,0:T(8,128)(2,1)S(1)}, u32[]{:S(2)}) copy-start(bf16[320,768]{1,0:T(8,128)(2,1)S(1)} %collective-permute-done.12.d2) | copy-start | bytes 1474564
  85.6 0.8 copy-start.6

commit v2 on v0

v2 whole, which is shorter than its diff:
```python
import functools

import jax
import jax.numpy as jnp
from jax import lax
from jax.experimental import pallas as pl
from jax.experimental.pallas import tpu as pltpu
from jax.sharding import Mesh, PartitionSpec as P

BLOCK = 128
LANES = 128
AXES = ("yh", "z", "x", "yl", "c")
SIZES = (2, 4, 4, 2, 2)
ROWS = ("yh", "z", "x", "yl", "c")
INST = ("yh", "z", "x")
TP = ("yl", "c")

beta_one = 0.9
beta_two = 0.999
adam_eps = 1e-08
step_rate = 0.02
decay_rate = 0.1
correct_one = 0.9999734386011124
correct_two = 0.09520785288629038
scale_eps = 1e-06

GATE_ROWS = 24
GATE_COLS = 1280
DOWN_ROWS = 10
DOWN_COLS = 3072
SHARE = 768
GATE_BLOCKS = GATE_COLS // BLOCK
DOWN_BLOCKS = SHARE // BLOCK
DOWN_LANE = 64


def index_of(yh, z, x, yl, c):
    return (((yh * 4 + z) * 4 + x) * 2 + yl) * 2 + c


def vmem():
    return pl.BlockSpec(memory_space=pltpu.VMEM)


def anywhere():
    return pl.BlockSpec(memory_space=pl.ANY)


def limit(mib):
    return pltpu.CompilerParams(vmem_limit_bytes=mib * 2**20)


def adamw_step(param, grad, moment, second):
    moment_new = beta_one * moment + (1.0 - beta_one) * grad
    second_new = beta_two * second + (1.0 - beta_two) * grad * grad
    update = moment_new / correct_one / (jnp.sqrt(second_new / correct_two) + adam_eps)
    param_new = param - step_rate * (update + decay_rate * param)
    return (param_new, moment_new, second_new)


def block_maxima(rows, first, row_count, blocks):
    size = jnp.abs(rows)
    below = lax.broadcasted_iota(jnp.int32, (row_count, 1), 0) < first
    out = []
    for part in (jnp.where(below, size, 0.0), jnp.where(below, 0.0, size)):
        top = jnp.max(part, axis=0, keepdims=True)
        tall = jnp.concatenate([top[:, k * BLOCK : (k + 1) * BLOCK] for k in range(blocks)], axis=0)
        out.append(jnp.max(tall, axis=1, keepdims=True))
    return out


def spread(low, high, blk, count, base):
    lane = lax.broadcasted_iota(jnp.int32, (1, LANES), 1) - base
    row = jnp.zeros((1, LANES), jnp.float32)
    for k in range(count):
        row = jnp.where(lane == blk * count + k, low[k : k + 1, :], row)
        row = jnp.where(lane == (blk + 1) * count + k, jnp.maximum(high[k : k + 1, :], row), row)
    return row


def adam_kernel(gp, gg, gm, gv, dp, dg, dm, dv, gpo, gmo, gvo, dpo, dmo, dvo, maxima):
    yh, z, x, yl, c = [lax.axis_index(name) for name in AXES]
    gate, gmo[...], gvo[...] = adamw_step(gp[...], gg[...], gm[...], gv[...])
    down, dmo[...], dvo[...] = adamw_step(dp[...], dg[...], dm[...], dv[...])
    gpo[...] = gate
    dpo[...] = down
    at = ((z % 2 * 4 + x) * 4 + yl * 2 + c) * GATE_ROWS
    blk = at // BLOCK
    low, high = block_maxima(gate, (blk + 1) * BLOCK - at, GATE_ROWS, GATE_BLOCKS)
    gate_row = spread(low, high, blk, GATE_BLOCKS, 0)
    at = index_of(yh, z, x, yl, c) * DOWN_ROWS
    blk = at // BLOCK
    low, high = block_maxima(down, (blk + 1) * BLOCK - at, DOWN_ROWS, 4 * DOWN_BLOCKS)
    rows = []
    for rank in range(4):
        part = slice(rank * DOWN_BLOCKS, (rank + 1) * DOWN_BLOCKS)
        row = spread(low[part], high[part], blk, DOWN_BLOCKS, DOWN_LANE)
        rows.append(jnp.where(yh * 2 + z // 2 == rank, jnp.maximum(row, gate_row), row))
    rows = jnp.concatenate(rows, axis=0)
    for i in range(16):
        maxima[i] = rows


def adam(gate, down):
    gate_shape = jax.ShapeDtypeStruct((GATE_ROWS, GATE_COLS), jnp.float32)
    down_shape = jax.ShapeDtypeStruct((DOWN_ROWS, DOWN_COLS), jnp.float32)
    return pl.pallas_call(
        adam_kernel,
        out_shape=(gate_shape,) * 3
        + (down_shape,) * 3
        + (jax.ShapeDtypeStruct((16, 4, LANES), jnp.float32),),
        in_specs=[vmem()] * 8,
        out_specs=(vmem(),) * 7,
    )(*gate, *down)


def slots_kernel(down, maxima, g0, g1, slots):
    rows = jnp.max(maxima[...], axis=0)
    for rank in range(4):
        for half in range(2):
            to = half * 4 + rank
            for k in range(DOWN_BLOCKS):
                col = slice(rank * SHARE + k * BLOCK, rank * SHARE + (k + 1) * BLOCK)
                slots[to, 8 * k : 8 * k + 8, :] = down[0:8, col]
                slots[to, 48 + 2 * k : 50 + 2 * k, :] = down[8:10, col]
            slots[to, 60:64, :] = jnp.broadcast_to(rows[rank : rank + 1], (4, LANES))


def make_slots(down, maxima, g0, g1):
    return pl.pallas_call(
        slots_kernel,
        out_shape=jax.ShapeDtypeStruct((8, 64, LANES), jnp.float32),
        in_specs=[vmem()] * 2 + [anywhere()] * 2,
        out_specs=vmem(),
        compiler_params=limit(2),
    )(down, maxima, g0, g1)


def quantize_kernel(g0, g1, slots, gate_out, down_out, scales, gate, down):
    yh, z, x = [lax.axis_index(name) for name in INST]
    gate[pl.ds(pl.multiple_of(yh * GATE_ROWS, 8), GATE_ROWS), :] = g0[...]
    gate[pl.ds(pl.multiple_of((1 - yh) * GATE_ROWS, 8), GATE_ROWS), :] = g1[...]
    for s in range(8):
        at = s * DOWN_ROWS
        for k in range(DOWN_BLOCKS):
            col = slice(k * BLOCK, (k + 1) * BLOCK)
            down[at : at + 8, col] = slots[s, 8 * k : 8 * k + 8, :]
            down[at + 8 : at + 10, col] = slots[s, 48 + 2 * k : 50 + 2 * k, :]
    lane = lax.broadcasted_iota(jnp.int32, (1, LANES), 1)
    top = jnp.max(jnp.max(slots[:, 60:64, :], axis=0), axis=0, keepdims=True) + scale_eps
    scales[...] = top

    def pick(at):
        return jnp.max(jnp.where(lane == at, top, 0.0), axis=1, keepdims=True)

    at = x * 96 + z // 2 * 48
    blk = at // BLOCK
    below = lax.broadcasted_iota(jnp.int32, (48, 1), 0) < (blk + 1) * BLOCK - at
    for k in range(GATE_BLOCKS):
        low = pick((3 * (z % 2) + blk) * GATE_BLOCKS + k)
        high = pick((3 * (z % 2) + blk + 1) * GATE_BLOCKS + k)
        col = slice(k * BLOCK, (k + 1) * BLOCK)
        gate_out[:, col] = (gate[:, col] / jnp.where(below, low, high)).astype(jnp.bfloat16)
    at = z * 160 + x * 40
    blk = at // BLOCK
    row = lax.broadcasted_iota(jnp.int32, (80, 1), 0)
    below = row % 40 < (blk + 1) * BLOCK - at
    for k in range(DOWN_BLOCKS):
        low, high = [
            jnp.where(
                row < 40,
                pick(DOWN_LANE + (blk + i) * DOWN_BLOCKS + k),
                pick(DOWN_LANE + (5 + blk + i) * DOWN_BLOCKS + k),
            )
            for i in range(2)
        ]
        col = slice(k * BLOCK, (k + 1) * BLOCK)
        down_out[:, col] = (down[:, col] / jnp.where(below, low, high)).astype(jnp.bfloat16)


def quantize(g0, g1, slots):
    return pl.pallas_call(
        quantize_kernel,
        out_shape=(
            jax.ShapeDtypeStruct((48, GATE_COLS), jnp.bfloat16),
            jax.ShapeDtypeStruct((80, SHARE), jnp.bfloat16),
            jax.ShapeDtypeStruct((1, LANES), jnp.float32),
        ),
        in_specs=[vmem()] * 3,
        out_specs=(vmem(),) * 3,
        scratch_shapes=[
            pltpu.VMEM((48, GATE_COLS), jnp.float32),
            pltpu.VMEM((80, SHARE), jnp.float32),
        ],
        compiler_params=limit(4),
    )(g0, g1, slots)


def pack_kernel(g0, g1, g2, g3, d0, d1, d2, d3, gate, down, rows):
    z, x = lax.axis_index("z"), lax.axis_index("x")
    for s, piece in enumerate((g0, g1, g2, g3)):
        zs = (z + 4 - s) % 4
        gate[pl.ds(pl.multiple_of((zs % 2) * 96 + (zs // 2) * 48, 16), 48), :] = piece[...]
    for s, piece in enumerate((d0, d1, d2, d3)):
        xs = (x + 4 - s) % 4
        wide = piece[...].astype(jnp.float32)
        for h in range(2):
            rows[pl.ds(pl.multiple_of(h * 160 + xs * 40, 8), 40), :] = wide[h * 40 : h * 40 + 40]
    down[...] = rows[...].astype(jnp.bfloat16)


def pack(gates, downs):
    return pl.pallas_call(
        pack_kernel,
        out_shape=(
            jax.ShapeDtypeStruct((192, GATE_COLS), jnp.bfloat16),
            jax.ShapeDtypeStruct((320, SHARE), jnp.bfloat16),
        ),
        in_specs=[vmem()] * 8,
        out_specs=(vmem(),) * 2,
        scratch_shapes=[pltpu.VMEM((320, SHARE), jnp.float32)],
        compiler_params=limit(6),
    )(*gates, *downs)


def place_kernel(axis, back, *refs):
    block, out, sems = refs[0], refs[-2], refs[-1]
    step = block.shape[0] // 2
    at = ((lax.axis_index(axis) + 4 - back) % 4) * step
    copies = [
        pltpu.make_async_copy(
            block.at[pl.ds(h * step, step), :],
            out.at[pl.ds(pl.multiple_of(h * 4 * step + at, 16), step), :],
            sems.at[h],
        )
        for h in range(2)
    ]
    for copy in copies:
        copy.start()
    for copy in copies:
        copy.wait()


def place(blocks, axis):
    rows, columns = blocks[0].shape
    out = ()
    for back in (0, 3, 2, 1):
        out = (
            pl.pallas_call(
                functools.partial(place_kernel, axis, back),
                out_shape=jax.ShapeDtypeStruct((rows * 4, columns), jnp.bfloat16),
                in_specs=[vmem()] + [anywhere()] * len(out),
                out_specs=anywhere(),
                input_output_aliases={1: 0} if out else {},
                scratch_shapes=[pltpu.SemaphoreType.DMA((2,))],
                compiler_params=limit(2),
            )(blocks[back], *out),
        )
    return out[0]


def gate_pairs(flip):
    pairs = []
    for yh in range(2):
        for z in range(4):
            for x in range(4):
                for yl in range(2):
                    for c in range(2):
                        target = index_of(c ^ flip, 2 * yl + z % 2, x, yh, z // 2)
                        pairs.append((index_of(yh, z, x, yl, c), target))
    return pairs


def around(array, axis):
    return [array] + [lax.ppermute(array, axis, [(i, (i + s) % 4) for i in range(4)]) for s in (1, 2, 3)]


def body(gate_param, gate_grad, gate_m, gate_v, down_param, down_grad, down_m, down_v):
    gate_new, gate_m_new, gate_v_new, down_new, down_m_new, down_v_new, maxima = adam(
        (gate_param, gate_grad, gate_m, gate_v), (down_param, down_grad, down_m, down_v)
    )
    g0 = lax.ppermute(gate_new, AXES, gate_pairs(0))
    g1 = lax.ppermute(gate_new, AXES, gate_pairs(1))
    maxima = lax.all_to_all(maxima, ("z", "x"), 0, 0, tiled=True)
    slots = make_slots(down_new, maxima, g0, g1)
    slots = lax.all_to_all(slots, ("yh", "yl", "c"), 0, 0, tiled=True)
    gate, down, scales = quantize(g0, g1, slots)
    gate, down = pack(around(gate, "z"), around(down, "x"))
    gate_quant = place(around(gate, "x"), "x")
    down_quant = place(around(down, "z"), "z")
    gate_scale = scales[0, :60].reshape(6, 10)
    down_scale = scales[0, DOWN_LANE : DOWN_LANE + 60].reshape(10, 6)
    return (
        gate_new,
        gate_m_new,
        gate_v_new,
        down_new,
        down_m_new,
        down_v_new,
        gate_quant[None],
        gate_scale[None],
        down_quant[None],
        down_scale[None],
    )


def solution(mesh):
    parts = Mesh(mesh.devices.reshape(SIZES), AXES)
    return jax.shard_map(
        body,
        mesh=parts,
        in_specs=(P(ROWS, None),) * 8,
        out_specs=(P(ROWS, None),) * 6
        + (
            P(INST, TP, None),
            P(INST, TP, None),
            P(INST, None, TP),
            P(INST, None, TP),
        ),
        check_vma=False,
    )
```

time: 492 us -> 78.9 us (0.16)
  waiting for transfers between devices: 406 us -> 18.3 us
  local copies, waits for them, and re-layouts: 46.2 us -> 3.21 us
  blocking collectives: 0 us -> 27.6 us
  other arithmetic: 24.8 us -> 0 us
  starting transfers between devices: 0.08 us -> 19.3 us
  between operations: 14.1 us -> 0.77 us
  Pallas kernels: 0 us -> 9.42 us
    all_gather x2 -> x0, waiting for transfers between devices: 406 us -> none  [the longest x1 229 us: down_plain_move(): whole = lax.all_gather(rows_piece, ('inst', 'tp'), axis=0, tiled=True)]
    unnamed x7, local copies, waits for them, and re-layouts: 30.3 us -> 2.38 us
    all_to_all x0 -> x2, blocking collectives: none -> 27.6 us  [the longest x1 16 us: body(): maxima = lax.all_to_all(maxima, ('z', 'x'), 0, 0, tiled=True)]
    ppermute x0 -> x14, starting transfers between devices: none -> 19.3 us  [the longest x12 13.6 us: around(): lax.ppermute(array, axis, [(i, (i + s) % 4) for i in range(4)])]
    ppermute x0 -> x14, waiting for transfers between devices: none -> 18.3 us  [the longest x12 18.3 us: around(): lax.ppermute(array, axis, [(i, (i + s) % 4) for i in range(4)])]
    abs x2 -> x0, local copies, waits for them, and re-layouts: 10.9 us -> none  [quantize(): block_max = jnp.max(jnp.abs(blocks), axis=(1, 3)) + scale_eps]
    pallas_call x0 -> x12, Pallas kernels: none -> 9.42 us  [the longest x8 6.42 us: place(): pl.pallas_call(functools.partial(place_kernel, axis, back), out_shape=jax...]
    abs x2 -> x0, other arithmetic: 8.84 us -> none  [quantize(): block_max = jnp.max(jnp.abs(blocks), axis=(1, 3)) + scale_eps]
  transfers between devices with their start and end apart: 2 -> 14, of which waited for: 2 -> 6; matrix products, arithmetic and copies ran while one was open for 8% -> 2% of each run, Pallas kernels for 0% -> 7%
where the time goes in v2:
time: 78.9 us; the launch traced here: 78.6 us
  blocking collectives  27.6 us (35%)
  starting transfers between devices  19.3 us (24%)
  waiting for transfers between devices  18.3 us (23%)
  Pallas kernels  9.42 us (12%)
  local copies, waits for them, and re-layouts  3.21 us (4%)
    ppermute x12, waiting for transfers between devices, around(): lax.ppermute(array, axis, [(i, (i + s) % 4) for i in range(4)])  18.3 us
    all_to_all x1, blocking collectives, body(): maxima = lax.all_to_all(maxima, ('z', 'x'), 0, 0, tiled=True)  16 us
    ppermute x12, starting transfers between devices, around(): lax.ppermute(array, axis, [(i, (i + s) % 4) for i in range(4)])  13.6 us
    all_to_all x1, blocking collectives, body(): slots = lax.all_to_all(slots, ('yh', 'yl', 'c'), 0, 0, tiled=True)  11.6 us
    pallas_call x8, Pallas kernels, place(): pl.pallas_call(functools.partial(place_kernel, axis, back), out_shape=jax...  6.42 us
    ppermute x1, starting transfers between devices, body(): g1 = lax.ppermute(gate_new, AXES, gate_pairs(1))  4.15 us
    pallas_call x1, Pallas kernels, adam(): pl.pallas_call(adam_kernel, out_shape=(gate_shape,) * 3 + (down_shape,) *...  2.62 us
    unnamed x7, local copies, waits for them, and re-layouts  2.38 us
  transfers between devices with their start and end apart: 14, of which 6 were waited for; matrix products, arithmetic and copies ran while one was open for 2% of the time, Pallas kernels for 7%

profile of v2, /device:TPU:0, one launch (start us, length us, event | category | flops | bytes accessed | tf_op | source)
XLA Modules:
  0.0 78.6 jit_solution(14749461299830228887)
XLA Ops:
  0.6 2.6 %shard_map.159 = (f32[24,1280]{1,0:T(8,128)}, f32[24,1280]{1,0:T(8,128)}, f32[24,1280]{1,0:T(8,128)}, f32[10,3072]{1,0:T(8,128)}, f32[10,3072]{1,0:T(8,128)}, /*index=5*/f32[10,3072]{1,0:T(8,128)}, f32[16,4,128]{2,1,0:T(4,128)}) custom-call(f32[24,1280]{1,0:T(8,128)} %gp.1, f32[24,1280]{1,0:T(8,128)} %gg.1, f32[24,1280]{1,0:T(8,128)} %gm.1, f32[24,1280]{1,0:T(8,128)} %gv.1, ...), custom_call_target="tpu_custom_call" | custom-call | tf_op jit(solution)/shard_map/pallas_call | solution.py:107
  3.3 1.5 %collective-permute-start = (f32[24,1280]{1,0:T(8,128)}, f32[24,1280]{1,0:T(8,128)S(1)}, u32[]{:S(2)}, u32[]{:S(2)}) collective-permute-start(f32[24,1280]{1,0:T(8,128)} %get-tuple-element.44), channel_id=1, source_target_pairs={{0,0},{1,64},{2,32},{3,96},{4,4},{5,68},{6,36},{7,100},{8,8},{9,72... | collective-permute-start | bytes 368648 | tf_op jit(solution)/shard_map/ppermute | solution.py:282
  4.8 4.1 %collective-permute-start.1 = (f32[24,1280]{1,0:T(8,128)}, f32[24,1280]{1,0:T(8,128)S(1)}, u32[]{:S(2)}, u32[]{:S(2)}) collective-permute-start(f32[24,1280]{1,0:T(8,128)} %get-tuple-element.44), channel_id=1, source_target_pairs={{0,64},{1,0},{2,96},{3,32},{4,68},{5,4},{6,100},{7,36},{8,72},{9,8... | collective-permute-start | bytes 368648 | tf_op jit(solution)/shard_map/ppermute | solution.py:283
  9.0 16.0 %all_to_all.10.maxima = f32[16,4,128]{2,1,0:T(4,128)S(1)} all-to-all(f32[16,4,128]{2,1,0:T(4,128)} %get-tuple-element.28), channel_id=1, replica_groups=mesh['yh'=2,'z'=4,'x'=4,'yl'=2,'c'=2] {'z','x'}, dimensions={0} | all-to-all | bytes 65536 | tf_op jit(solution)/shard_map/all_to_all | solution.py:284
  25.0 0.9 %copy-done.2 = f32[10,3072]{1,0:T(8,128)S(1)} copy-done((f32[10,3072]{1,0:T(8,128)S(1)}, f32[10,3072]{1,0:T(8,128)}, u32[]{:S(2)}) %copy-start.2) | copy-done | bytes 122904
  26.0 11.6 %all_to_all.11.slots = f32[8,64,128]{2,1,0:T(8,128)S(1)} all-to-all(f32[8,64,128]{2,1,0:T(8,128)S(1)} %shard_map.160), channel_id=1, replica_groups=mesh['yh'=2,'z'=4,'x'=4,'yl'=2,'c'=2] {'yh','yl','c'}, dimensions={0} | all-to-all | bytes 524288 | tf_op jit(solution)/shard_map/all_to_all | solution.py:286
  37.7 0.6 collective-permute-start.2
  38.4 2.1 %collective-permute-start.3 = (bf16[48,1280]{1,0:T(8,128)(2,1)S(1)}, bf16[48,1280]{1,0:T(8,128)(2,1)S(1)}, u32[]{:S(2)}, u32[]{:S(2)}) collective-permute-start(bf16[48,1280]{1,0:T(8,128)(2,1)S(1)} %get-tuple-element.29.g0), channel_id=1, source_target_pairs={{0,32},{16,48},{32,0},{48,16},{1,33},{17,49},{33,1},{49,17},{2,34}... | collective-permute-start | bytes 368648 | tf_op jit(solution)/shard_map/ppermute | solution.py:275
  40.4 1.2 %collective-permute-start.4 = (bf16[48,1280]{1,0:T(8,128)(2,1)S(1)}, bf16[48,1280]{1,0:T(8,128)(2,1)S(1)}, u32[]{:S(2)}, u32[]{:S(2)}) collective-permute-start(bf16[48,1280]{1,0:T(8,128)(2,1)S(1)} %get-tuple-element.29.g0), channel_id=1, source_target_pairs={{0,48},{16,0},{32,16},{48,32},{1,49},{17,1},{33,17},{49,33},{2,50}... | collective-permute-start | bytes 368648 | tf_op jit(solution)/shard_map/ppermute | solution.py:275
  41.6 0.6 collective-permute-start.5
  42.2 2.1 %collective-permute-start.6 = (bf16[80,768]{1,0:T(8,128)(2,1)S(1)}, bf16[80,768]{1,0:T(8,128)(2,1)S(1)}, u32[]{:S(2)}, u32[]{:S(2)}) collective-permute-start(bf16[80,768]{1,0:T(8,128)(2,1)S(1)} %get-tuple-element.30.d0), channel_id=1, source_target_pairs={{0,8},{4,12},{8,0},{12,4},{1,9},{5,13},{9,1},{13,5},{2,10},{6,14},... | collective-permute-start | bytes 368648 | tf_op jit(solution)/shard_map/ppermute | solution.py:275
  44.3 2.1 %collective-permute-done.2.g1 = bf16[48,1280]{1,0:T(8,128)(2,1)S(1)} collective-permute-done((bf16[48,1280]{1,0:T(8,128)(2,1)S(1)}, bf16[48,1280]{1,0:T(8,128)(2,1)S(1)}, u32[]{:S(2)}, u32[]{:S(2)}) %collective-permute-start.2) | collective-permute-done | bytes 122912 | tf_op jit(solution)/shard_map/ppermute | solution.py:275
  46.3 1.2 %collective-permute-start.7 = (bf16[80,768]{1,0:T(8,128)(2,1)S(1)}, bf16[80,768]{1,0:T(8,128)(2,1)S(1)}, u32[]{:S(2)}, u32[]{:S(2)}) collective-permute-start(bf16[80,768]{1,0:T(8,128)(2,1)S(1)} %get-tuple-element.30.d0), channel_id=1, source_target_pairs={{0,12},{4,0},{8,4},{12,8},{1,13},{5,1},{9,5},{13,9},{2,14},{6,2},{... | collective-permute-start | bytes 368648 | tf_op jit(solution)/shard_map/ppermute | solution.py:275
  47.5 1.8 %collective-permute-done.5.d1 = bf16[80,768]{1,0:T(8,128)(2,1)S(1)} collective-permute-done((bf16[80,768]{1,0:T(8,128)(2,1)S(1)}, bf16[80,768]{1,0:T(8,128)(2,1)S(1)}, u32[]{:S(2)}, u32[]{:S(2)}) %collective-permute-start.5) | collective-permute-done | bytes 122912 | tf_op jit(solution)/shard_map/ppermute | solution.py:275
  49.3 1.9 %collective-permute-done.7.d3 = bf16[80,768]{1,0:T(8,128)(2,1)S(1)} collective-permute-done((bf16[80,768]{1,0:T(8,128)(2,1)S(1)}, bf16[80,768]{1,0:T(8,128)(2,1)S(1)}, u32[]{:S(2)}, u32[]{:S(2)}) %collective-permute-start.7) | collective-permute-done | bytes 122912 | tf_op jit(solution)/shard_map/ppermute | solution.py:275
  51.5 1.6 %collective-permute-start.12 = (bf16[320,768]{1,0:T(8,128)(2,1)S(1)}, bf16[320,768]{1,0:T(8,128)(2,1)S(1)}, u32[]{:S(2)}, u32[]{:S(2)}) collective-permute-start(bf16[320,768]{1,0:T(8,128)(2,1)S(1)} %get-tuple-element.33.refs_0_), channel_id=1, source_target_pairs={{0,32},{16,48},{32,0},{48,16},{1,33},{17,49},{33,1},{49,17},{2,34}... | collective-permute-start | bytes 1474568 | tf_op jit(solution)/shard_map/ppermute | solution.py:275
  53.0 0.9 %collective-permute-start.11 = (bf16[320,768]{1,0:T(8,128)(2,1)S(1)}, bf16[320,768]{1,0:T(8,128)(2,1)S(1)}, u32[]{:S(2)}, u32[]{:S(2)}) collective-permute-start(bf16[320,768]{1,0:T(8,128)(2,1)S(1)} %get-tuple-element.33.refs_0_), channel_id=1, source_target_pairs={{0,16},{16,32},{32,48},{48,0},{1,17},{17,33},{33,49},{49,1},{2,18}... | collective-permute-start | bytes 1474568 | tf_op jit(solution)/shard_map/ppermute | solution.py:275
  53.9 2.7 %collective-permute-start.10 = (bf16[192,1280]{1,0:T(8,128)(2,1)S(1)}, bf16[192,1280]{1,0:T(8,128)(2,1)S(1)}, u32[]{:S(2)}, u32[]{:S(2)}) collective-permute-start(bf16[192,1280]{1,0:T(8,128)(2,1)S(1)} %get-tuple-element.31.refs_0_), channel_id=1, source_target_pairs={{0,12},{4,0},{8,4},{12,8},{1,13},{5,1},{9,5},{13,9},{2,14},{6,2},{... | collective-permute-start | bytes 1474568 | tf_op jit(solution)/shard_map/ppermute | solution.py:275
  56.7 8.9 %collective-permute-done.13.refs_0_ = bf16[320,768]{1,0:T(8,128)(2,1)S(1)} collective-permute-done((bf16[320,768]{1,0:T(8,128)(2,1)S(1)}, bf16[320,768]{1,0:T(8,128)(2,1)S(1)}, u32[]{:S(2)}, u32[]{:S(2)}) %collective-permute-start.13) | collective-permute-done | bytes 491552 | tf_op jit(solution)/shard_map/ppermute | solution.py:275
  65.6 0.8 copy-done
  67.1 0.7 copy.27
  67.8 0.7 broadcast_in_dim_reshape_squeeze.8
  68.5 0.8 %shard_map.167.refs_1_ = bf16[1280,768]{1,0:T(8,128)(2,1)} custom-call(bf16[320,768]{1,0:T(8,128)(2,1)S(1)} %get-tuple-element.33.refs_0_), custom_call_target="tpu_custom_call" | custom-call | tf_op jit(solution)/shard_map/pallas_call | solution.py:249
  69.3 0.8 %shard_map.163.refs_1_ = bf16[768,1280]{1,0:T(8,128)(2,1)} custom-call(bf16[192,1280]{1,0:T(8,128)(2,1)S(1)} %get-tuple-element.31.refs_0_), custom_call_target="tpu_custom_call" | custom-call | tf_op jit(solution)/shard_map/pallas_call | solution.py:249
  70.1 0.8 %shard_map.168.refs_1_ = bf16[1280,768]{1,0:T(8,128)(2,1)} custom-call(bf16[320,768]{1,0:T(8,128)(2,1)S(1)} %copy-done.1, bf16[1280,768]{1,0:T(8,128)(2,1)} %shard_map.167.refs_1_), custom_call_target="tpu_custom_call", output_to_operand_aliasing={{}: (1, {})} | custom-call | tf_op jit(solution)/shard_map/pallas_call | solution.py:249
  70.9 0.8 %shard_map.169.refs_1_ = bf16[1280,768]{1,0:T(8,128)(2,1)} custom-call(bf16[320,768]{1,0:T(8,128)(2,1)S(1)} %collective-permute-done.12.refs_0_, bf16[1280,768]{1,0:T(8,128)(2,1)} %shard_map.168.refs_1_), custom_call_target="tpu_custom_call", output_to_operand_aliasing={{}: (1, {})} | custom-call | tf_op jit(solution)/shard_map/pallas_call | solution.py:249
  71.7 2.4 %collective-permute-done.11.refs_0_ = bf16[320,768]{1,0:T(8,128)(2,1)S(1)} collective-permute-done((bf16[320,768]{1,0:T(8,128)(2,1)S(1)}, bf16[320,768]{1,0:T(8,128)(2,1)S(1)}, u32[]{:S(2)}, u32[]{:S(2)}) %collective-permute-start.11) | collective-permute-done | bytes 491552 | tf_op jit(solution)/shard_map/ppermute | solution.py:275
  74.1 0.8 %shard_map.170 = bf16[1280,768]{1,0:T(8,128)(2,1)} custom-call(bf16[320,768]{1,0:T(8,128)(2,1)S(1)} %collective-permute-done.11.refs_0_, bf16[1280,768]{1,0:T(8,128)(2,1)} %shard_map.169.refs_1_), custom_call_target="tpu_custom_call", output_to_operand_aliasing={{}: (1, {})} | custom-call | tf_op jit(solution)/shard_map/pallas_call | solution.py:249
  74.9 0.8 %shard_map.164.refs_1_ = bf16[768,1280]{1,0:T(8,128)(2,1)} custom-call(bf16[192,1280]{1,0:T(8,128)(2,1)S(1)} %collective-permute-done.10.refs_0_, bf16[768,1280]{1,0:T(8,128)(2,1)} %shard_map.163.refs_1_), custom_call_target="tpu_custom_call", output_to_operand_aliasing={{}: (1, {})} | custom-call | tf_op jit(solution)/shard_map/pallas_call | solution.py:249
  75.8 0.8 %shard_map.165.refs_1_ = bf16[768,1280]{1,0:T(8,128)(2,1)} custom-call(bf16[192,1280]{1,0:T(8,128)(2,1)S(1)} %collective-permute-done.9.refs_0_, bf16[768,1280]{1,0:T(8,128)(2,1)} %shard_map.164.refs_1_), custom_call_target="tpu_custom_call", output_to_operand_aliasing={{}: (1, {})} | custom-call | tf_op jit(solution)/shard_map/pallas_call | solution.py:249
  76.6 1.2 %collective-permute-done.8.refs_0_ = bf16[192,1280]{1,0:T(8,128)(2,1)S(1)} collective-permute-done((bf16[192,1280]{1,0:T(8,128)(2,1)S(1)}, bf16[192,1280]{1,0:T(8,128)(2,1)S(1)}, u32[]{:S(2)}, u32[]{:S(2)}) %collective-permute-start.8) | collective-permute-done | bytes 491552 | tf_op jit(solution)/shard_map/ppermute | solution.py:275
  77.8 0.8 %shard_map.166 = bf16[768,1280]{1,0:T(8,128)(2,1)} custom-call(bf16[192,1280]{1,0:T(8,128)(2,1)S(1)} %collective-permute-done.8.refs_0_, bf16[768,1280]{1,0:T(8,128)(2,1)} %shard_map.165.refs_1_), custom_call_target="tpu_custom_call", output_to_operand_aliasing={{}: (1, {})} | custom-call | tf_op jit(solution)/shard_map/pallas_call | solution.py:249
  (20 shorter events, 1.3 us)
Async XLA Ops:
  3.3 21.7 %collective-permute-start = (f32[24,1280]{1,0:T(8,128)}, f32[24,1280]{1,0:T(8,128)S(1)}, u32[]{:S(2)}, u32[]{:S(2)}) collective-permute-start(f32[24,1280]{1,0:T(8,128)} %get-tuple-element.44), channel_id=1, source_target_pairs={{0,0},{1,64},{2,32},{3,96},{4,4},{5,68},{6,36},{7,100},{8,8},{9,72... | collective-permute-start | bytes 368648 | tf_op jit(solution)/shard_map/ppermute | solution.py:282
  4.8 20.2 %collective-permute-start.1 = (f32[24,1280]{1,0:T(8,128)}, f32[24,1280]{1,0:T(8,128)S(1)}, u32[]{:S(2)}, u32[]{:S(2)}) collective-permute-start(f32[24,1280]{1,0:T(8,128)} %get-tuple-element.44), channel_id=1, source_target_pairs={{0,64},{1,0},{2,96},{3,32},{4,68},{5,4},{6,100},{7,36},{8,72},{9,8... | collective-permute-start | bytes 368648 | tf_op jit(solution)/shard_map/ppermute | solution.py:283
  25.0 0.9 %copy-start.2 = (f32[10,3072]{1,0:T(8,128)S(1)}, f32[10,3072]{1,0:T(8,128)}, u32[]{:S(2)}) copy-start(f32[10,3072]{1,0:T(8,128)} %get-tuple-element.47.down) | copy-start | bytes 368644
  37.7 8.6 %collective-permute-start.2 = (bf16[48,1280]{1,0:T(8,128)(2,1)S(1)}, bf16[48,1280]{1,0:T(8,128)(2,1)S(1)}, u32[]{:S(2)}, u32[]{:S(2)}) collective-permute-start(bf16[48,1280]{1,0:T(8,128)(2,1)S(1)} %get-tuple-element.29.g0), channel_id=1, source_target_pairs={{0,16},{16,32},{32,48},{48,0},{1,17},{17,33},{33,49},{49,1},{2,18}... | collective-permute-start | bytes 368648 | tf_op jit(solution)/shard_map/ppermute | solution.py:275
  38.4 9.2 %collective-permute-start.3 = (bf16[48,1280]{1,0:T(8,128)(2,1)S(1)}, bf16[48,1280]{1,0:T(8,128)(2,1)S(1)}, u32[]{:S(2)}, u32[]{:S(2)}) collective-permute-start(bf16[48,1280]{1,0:T(8,128)(2,1)S(1)} %get-tuple-element.29.g0), channel_id=1, source_target_pairs={{0,32},{16,48},{32,0},{48,16},{1,33},{17,49},{33,1},{49,17},{2,34}... | collective-permute-start | bytes 368648 | tf_op jit(solution)/shard_map/ppermute | solution.py:275
  40.4 7.1 %collective-permute-start.4 = (bf16[48,1280]{1,0:T(8,128)(2,1)S(1)}, bf16[48,1280]{1,0:T(8,128)(2,1)S(1)}, u32[]{:S(2)}, u32[]{:S(2)}) collective-permute-start(bf16[48,1280]{1,0:T(8,128)(2,1)S(1)} %get-tuple-element.29.g0), channel_id=1, source_target_pairs={{0,48},{16,0},{32,16},{48,32},{1,49},{17,1},{33,17},{49,33},{2,50}... | collective-permute-start | bytes 368648 | tf_op jit(solution)/shard_map/ppermute | solution.py:275
  41.6 7.7 %collective-permute-start.5 = (bf16[80,768]{1,0:T(8,128)(2,1)S(1)}, bf16[80,768]{1,0:T(8,128)(2,1)S(1)}, u32[]{:S(2)}, u32[]{:S(2)}) collective-permute-start(bf16[80,768]{1,0:T(8,128)(2,1)S(1)} %get-tuple-element.30.d0), channel_id=1, source_target_pairs={{0,4},{4,8},{8,12},{12,0},{1,5},{5,9},{9,13},{13,1},{2,6},{6,10},{... | collective-permute-start | bytes 368648 | tf_op jit(solution)/shard_map/ppermute | solution.py:275
  42.2 7.1 %collective-permute-start.6 = (bf16[80,768]{1,0:T(8,128)(2,1)S(1)}, bf16[80,768]{1,0:T(8,128)(2,1)S(1)}, u32[]{:S(2)}, u32[]{:S(2)}) collective-permute-start(bf16[80,768]{1,0:T(8,128)(2,1)S(1)} %get-tuple-element.30.d0), channel_id=1, source_target_pairs={{0,8},{4,12},{8,0},{12,4},{1,9},{5,13},{9,1},{13,5},{2,10},{6,14},... | collective-permute-start | bytes 368648 | tf_op jit(solution)/shard_map/ppermute | solution.py:275
  46.3 4.9 %collective-permute-start.7 = (bf16[80,768]{1,0:T(8,128)(2,1)S(1)}, bf16[80,768]{1,0:T(8,128)(2,1)S(1)}, u32[]{:S(2)}, u32[]{:S(2)}) collective-permute-start(bf16[80,768]{1,0:T(8,128)(2,1)S(1)} %get-tuple-element.30.d0), channel_id=1, source_target_pairs={{0,12},{4,0},{8,4},{12,8},{1,13},{5,1},{9,5},{13,9},{2,14},{6,2},{... | collective-permute-start | bytes 368648 | tf_op jit(solution)/shard_map/ppermute | solution.py:275
  51.4 14.2 %collective-permute-start.13 = (bf16[320,768]{1,0:T(8,128)(2,1)S(1)}, bf16[320,768]{1,0:T(8,128)(2,1)S(1)}, u32[]{:S(2)}, u32[]{:S(2)}) collective-permute-start(bf16[320,768]{1,0:T(8,128)(2,1)S(1)} %get-tuple-element.33.refs_0_), channel_id=1, source_target_pairs={{0,48},{16,0},{32,16},{48,32},{1,49},{17,1},{33,17},{49,33},{2,50}... | collective-permute-start | bytes 1474568 | tf_op jit(solution)/shard_map/ppermute | solution.py:275
  51.5 19.4 %collective-permute-start.12 = (bf16[320,768]{1,0:T(8,128)(2,1)S(1)}, bf16[320,768]{1,0:T(8,128)(2,1)S(1)}, u32[]{:S(2)}, u32[]{:S(2)}) collective-permute-start(bf16[320,768]{1,0:T(8,128)(2,1)S(1)} %get-tuple-element.33.refs_0_), channel_id=1, source_target_pairs={{0,32},{16,48},{32,0},{48,16},{1,33},{17,49},{33,1},{49,17},{2,34}... | collective-permute-start | bytes 1474568 | tf_op jit(solution)/shard_map/ppermute | solution.py:275
  53.0 21.1 %collective-permute-start.11 = (bf16[320,768]{1,0:T(8,128)(2,1)S(1)}, bf16[320,768]{1,0:T(8,128)(2,1)S(1)}, u32[]{:S(2)}, u32[]{:S(2)}) collective-permute-start(bf16[320,768]{1,0:T(8,128)(2,1)S(1)} %get-tuple-element.33.refs_0_), channel_id=1, source_target_pairs={{0,16},{16,32},{32,48},{48,0},{1,17},{17,33},{33,49},{49,1},{2,18}... | collective-permute-start | bytes 1474568 | tf_op jit(solution)/shard_map/ppermute | solution.py:275
  53.9 21.0 %collective-permute-start.10 = (bf16[192,1280]{1,0:T(8,128)(2,1)S(1)}, bf16[192,1280]{1,0:T(8,128)(2,1)S(1)}, u32[]{:S(2)}, u32[]{:S(2)}) collective-permute-start(bf16[192,1280]{1,0:T(8,128)(2,1)S(1)} %get-tuple-element.31.refs_0_), channel_id=1, source_target_pairs={{0,12},{4,0},{8,4},{12,8},{1,13},{5,1},{9,5},{13,9},{2,14},{6,2},{... | collective-permute-start | bytes 1474568 | tf_op jit(solution)/shard_map/ppermute | solution.py:275
  56.6 19.2 %collective-permute-start.9 = (bf16[192,1280]{1,0:T(8,128)(2,1)S(1)}, bf16[192,1280]{1,0:T(8,128)(2,1)S(1)}, u32[]{:S(2)}, u32[]{:S(2)}) collective-permute-start(bf16[192,1280]{1,0:T(8,128)(2,1)S(1)} %get-tuple-element.31.refs_0_), channel_id=1, source_target_pairs={{0,8},{4,12},{8,0},{12,4},{1,9},{5,13},{9,1},{13,5},{2,10},{6,14},... | collective-permute-start | bytes 1474568 | tf_op jit(solution)/shard_map/ppermute | solution.py:275
  65.6 0.8 copy-start
  66.4 11.4 %collective-permute-start.8 = (bf16[192,1280]{1,0:T(8,128)(2,1)S(1)}, bf16[192,1280]{1,0:T(8,128)(2,1)S(1)}, u32[]{:S(2)}, u32[]{:S(2)}) collective-permute-start(bf16[192,1280]{1,0:T(8,128)(2,1)S(1)} %get-tuple-element.31.refs_0_), channel_id=1, source_target_pairs={{0,4},{4,8},{8,12},{12,0},{1,5},{5,9},{9,13},{13,1},{2,6},{6,10},{... | collective-permute-start | bytes 1474568 | tf_op jit(solution)/shard_map/ppermute | solution.py:275
  68.5 1.6 %copy-start.1 = (bf16[320,768]{1,0:T(8,128)(2,1)S(1)}, bf16[320,768]{1,0:T(8,128)(2,1)}, u32[]{:S(2)}) copy-start(bf16[320,768]{1,0:T(8,128)(2,1)} %copy-done) | copy-start | bytes 1474564

commit v3 on v2

--- a/solution.py
+++ b/solution.py
@@ -56,6 +56,33 @@
     update = moment_new / correct_one / (jnp.sqrt(second_new / correct_two) + adam_eps)
     param_new = param - step_rate * (update + decay_rate * param)
     return (param_new, moment_new, second_new)
+
+
+def adam_kernel(gp, gg, gm, gv, dp, dg, dm, dv, gpo, gmo, gvo, dpo, dmo, dvo, slots):
+    gpo[...], gmo[...], gvo[...] = adamw_step(gp[...], gg[...], gm[...], gv[...])
+    down, dmo[...], dvo[...] = adamw_step(dp[...], dg[...], dm[...], dv[...])
+    dpo[...] = down
+    for rank in range(4):
+        for k in range(DOWN_BLOCKS):
+            col = rank * SHARE + k * BLOCK
+            for half in range(2):
+                slots[half * 4 + rank, 8 * k : 8 * k + 8, :] = down[0:8, col : col + BLOCK]
+                slots[half * 4 + rank, 48 + 2 * k : 50 + 2 * k, :] = down[8:10, col : col + BLOCK]
+        for half in range(2):
+            slots[half * 4 + rank, 60:64, :] = jnp.zeros((4, LANES), jnp.float32)
+
+
+def adam(gate, down):
+    gate_shape = jax.ShapeDtypeStruct((GATE_ROWS, GATE_COLS), jnp.float32)
+    down_shape = jax.ShapeDtypeStruct((DOWN_ROWS, DOWN_COLS), jnp.float32)
+    return pl.pallas_call(
+        adam_kernel,
+        out_shape=(gate_shape,) * 3
+        + (down_shape,) * 3
+        + (jax.ShapeDtypeStruct((8, 64, LANES), jnp.float32),),
+        in_specs=[vmem()] * 8,
+        out_specs=(vmem(),) * 7,
+    )(*gate, *down)
 
 
 def block_maxima(rows, first, row_count, blocks):
@@ -78,65 +105,7 @@
     return row
 
 
-def adam_kernel(gp, gg, gm, gv, dp, dg, dm, dv, gpo, gmo, gvo, dpo, dmo, dvo, maxima):
-    yh, z, x, yl, c = [lax.axis_index(name) for name in AXES]
-    gate, gmo[...], gvo[...] = adamw_step(gp[...], gg[...], gm[...], gv[...])
-    down, dmo[...], dvo[...] = adamw_step(dp[...], dg[...], dm[...], dv[...])
-    gpo[...] = gate
-    dpo[...] = down
-    at = ((z % 2 * 4 + x) * 4 + yl * 2 + c) * GATE_ROWS
-    blk = at // BLOCK
-    low, high = block_maxima(gate, (blk + 1) * BLOCK - at, GATE_ROWS, GATE_BLOCKS)
-    gate_row = spread(low, high, blk, GATE_BLOCKS, 0)
-    at = index_of(yh, z, x, yl, c) * DOWN_ROWS
-    blk = at // BLOCK
-    low, high = block_maxima(down, (blk + 1) * BLOCK - at, DOWN_ROWS, 4 * DOWN_BLOCKS)
-    rows = []
-    for rank in range(4):
-        part = slice(rank * DOWN_BLOCKS, (rank + 1) * DOWN_BLOCKS)
-        row = spread(low[part], high[part], blk, DOWN_BLOCKS, DOWN_LANE)
-        rows.append(jnp.where(yh * 2 + z // 2 == rank, jnp.maximum(row, gate_row), row))
-    rows = jnp.concatenate(rows, axis=0)
-    for i in range(16):
-        maxima[i] = rows
-
-
-def adam(gate, down):
-    gate_shape = jax.ShapeDtypeStruct((GATE_ROWS, GATE_COLS), jnp.float32)
-    down_shape = jax.ShapeDtypeStruct((DOWN_ROWS, DOWN_COLS), jnp.float32)
-    return pl.pallas_call(
-        adam_kernel,
-        out_shape=(gate_shape,) * 3
-        + (down_shape,) * 3
-        + (jax.ShapeDtypeStruct((16, 4, LANES), jnp.float32),),
-        in_specs=[vmem()] * 8,
-        out_specs=(vmem(),) * 7,
-    )(*gate, *down)
-
-
-def slots_kernel(down, maxima, g0, g1, slots):
-    rows = jnp.max(maxima[...], axis=0)
-    for rank in range(4):
-        for half in range(2):
-            to = half * 4 + rank
-            for k in range(DOWN_BLOCKS):
-                col = slice(rank * SHARE + k * BLOCK, rank * SHARE + (k + 1) * BLOCK)
-                slots[to, 8 * k : 8 * k + 8, :] = down[0:8, col]
-                slots[to, 48 + 2 * k : 50 + 2 * k, :] = down[8:10, col]
-            slots[to, 60:64, :] = jnp.broadcast_to(rows[rank : rank + 1], (4, LANES))
-
-
-def make_slots(down, maxima, g0, g1):
-    return pl.pallas_call(
-        slots_kernel,
-        out_shape=jax.ShapeDtypeStruct((8, 64, LANES), jnp.float32),
-        in_specs=[vmem()] * 2 + [anywhere()] * 2,
-        out_specs=vmem(),
-        compiler_params=limit(2),
-    )(down, maxima, g0, g1)
-
-
-def quantize_kernel(g0, g1, slots, gate_out, down_out, scales, gate, down):
+def unpack_kernel(g0, g1, slots, gate, down, maxima):
     yh, z, x = [lax.axis_index(name) for name in INST]
     gate[pl.ds(pl.multiple_of(yh * GATE_ROWS, 8), GATE_ROWS), :] = g0[...]
     gate[pl.ds(pl.multiple_of((1 - yh) * GATE_ROWS, 8), GATE_ROWS), :] = g1[...]
@@ -146,8 +115,37 @@
             col = slice(k * BLOCK, (k + 1) * BLOCK)
             down[at : at + 8, col] = slots[s, 8 * k : 8 * k + 8, :]
             down[at + 8 : at + 10, col] = slots[s, 48 + 2 * k : 50 + 2 * k, :]
+    at = x * 96 + z // 2 * 48
+    blk = at // BLOCK
+    low, high = block_maxima(gate[...], (blk + 1) * BLOCK - at, 48, GATE_BLOCKS)
+    row = spread(low, high, 3 * (z % 2) + blk, GATE_BLOCKS, 0)
+    at = z * 160 + x * 40
+    blk = at // BLOCK
+    for h in range(2):
+        low, high = block_maxima(down[h * 40 : h * 40 + 40, :], (blk + 1) * BLOCK - at, 40, DOWN_BLOCKS)
+        row = jnp.maximum(row, spread(low, high, 5 * h + blk, DOWN_BLOCKS, DOWN_LANE))
+    for i in range(16):
+        maxima[i] = row
+
+
+def unpack(g0, g1, slots):
+    return pl.pallas_call(
+        unpack_kernel,
+        out_shape=(
+            jax.ShapeDtypeStruct((48, GATE_COLS), jnp.float32),
+            jax.ShapeDtypeStruct((80, SHARE), jnp.float32),
+            jax.ShapeDtypeStruct((16, 1, LANES), jnp.float32),
+        ),
+        in_specs=[vmem()] * 3,
+        out_specs=(vmem(),) * 3,
+        compiler_params=limit(4),
+    )(g0, g1, slots)
+
+
+def quantize_kernel(gate, down, maxima, gate_out, down_out, scales):
+    yh, z, x = [lax.axis_index(name) for name in INST]
     lane = lax.broadcasted_iota(jnp.int32, (1, LANES), 1)
-    top = jnp.max(jnp.max(slots[:, 60:64, :], axis=0), axis=0, keepdims=True) + scale_eps
+    top = jnp.max(maxima[...], axis=0) + scale_eps
     scales[...] = top
 
     def pick(at):
@@ -178,7 +176,7 @@
         down_out[:, col] = (down[:, col] / jnp.where(below, low, high)).astype(jnp.bfloat16)
 
 
-def quantize(g0, g1, slots):
+def quantize(gate, down, maxima):
     return pl.pallas_call(
         quantize_kernel,
         out_shape=(
@@ -188,12 +186,8 @@
         ),
         in_specs=[vmem()] * 3,
         out_specs=(vmem(),) * 3,
-        scratch_shapes=[
-            pltpu.VMEM((48, GATE_COLS), jnp.float32),
-            pltpu.VMEM((80, SHARE), jnp.float32),
-        ],
         compiler_params=limit(4),
-    )(g0, g1, slots)
+    )(gate, down, maxima)
 
 
 def pack_kernel(g0, g1, g2, g3, d0, d1, d2, d3, gate, down, rows):
@@ -244,7 +238,7 @@
 def place(blocks, axis):
     rows, columns = blocks[0].shape
     out = ()
-    for back in (0, 3, 2, 1):
+    for back in (0, 1, 3, 2):
         out = (
             pl.pallas_call(
                 functools.partial(place_kernel, axis, back),
@@ -271,23 +265,32 @@
     return pairs
 
 
+def shift(array, axis, by):
+    return lax.ppermute(array, axis, [(i, (i + by) % 4) for i in range(4)])
+
+
 def around(array, axis):
-    return [array] + [lax.ppermute(array, axis, [(i, (i + s) % 4) for i in range(4)]) for s in (1, 2, 3)]
+    return [array] + [shift(array, axis, by) for by in (1, 2, 3)]
+
+
+def around_by_neighbours(array, axis):
+    back = shift(array, axis, 1)
+    return [array, back, shift(back, axis, 1), shift(array, axis, 3)]
 
 
 def body(gate_param, gate_grad, gate_m, gate_v, down_param, down_grad, down_m, down_v):
-    gate_new, gate_m_new, gate_v_new, down_new, down_m_new, down_v_new, maxima = adam(
+    gate_new, gate_m_new, gate_v_new, down_new, down_m_new, down_v_new, slots = adam(
         (gate_param, gate_grad, gate_m, gate_v), (down_param, down_grad, down_m, down_v)
     )
     g0 = lax.ppermute(gate_new, AXES, gate_pairs(0))
     g1 = lax.ppermute(gate_new, AXES, gate_pairs(1))
+    slots = lax.all_to_all(slots, ("yh", "yl", "c"), 0, 0, tiled=True)
+    gate, down, maxima = unpack(g0, g1, slots)
     maxima = lax.all_to_all(maxima, ("z", "x"), 0, 0, tiled=True)
-    slots = make_slots(down_new, maxima, g0, g1)
-    slots = lax.all_to_all(slots, ("yh", "yl", "c"), 0, 0, tiled=True)
-    gate, down, scales = quantize(g0, g1, slots)
+    gate, down, scales = quantize(gate, down, maxima)
     gate, down = pack(around(gate, "z"), around(down, "x"))
-    gate_quant = place(around(gate, "x"), "x")
-    down_quant = place(around(down, "z"), "z")
+    gate_quant = place(around_by_neighbours(gate, "x"), "x")
+    down_quant = place(around_by_neighbours(down, "z"), "z")
     gate_scale = scales[0, :60].reshape(6, 10)
     down_scale = scales[0, DOWN_LANE : DOWN_LANE + 60].reshape(10, 6)
     return (

time: 78.9 us -> 72.8 us (0.923)
  the two profiles are of different devices: /device:TPU:0 before, /device:TPU:16 now
where the time goes in v3:
time: 72.8 us; the launch traced here: 72.4 us
  starting transfers between devices  27.1 us (37%)
  blocking collectives  16.4 us (23%)
  waiting for transfers between devices  16.1 us (22%)
  Pallas kernels  10.6 us (15%)
  local copies, waits for them, and re-layouts  1.5 us (2%)
  between operations  0.75 us (1%)
    all_to_all x1, blocking collectives, body(): maxima = lax.all_to_all(maxima, ('z', 'x'), 0, 0, tiled=True)  16.4 us
    ppermute x12, starting transfers between devices, shift(): return lax.ppermute(array, axis, [(i, (i + by) % 4) for i in range(4)])  14.3 us
    ppermute x12, waiting for transfers between devices, shift(): return lax.ppermute(array, axis, [(i, (i + by) % 4) for i in range(4)])  13.3 us
    pallas_call x8, Pallas kernels, place(): pl.pallas_call(functools.partial(place_kernel, axis, back), out_shape=jax...  7.43 us
    ppermute x1, starting transfers between devices, body(): g1 = lax.ppermute(gate_new, AXES, gate_pairs(1))  5.45 us
    all_to_all x1, starting transfers between devices, body(): slots = lax.all_to_all(slots, ('yh', 'yl', 'c'), 0, 0, tiled=True)  4.8 us
    ppermute x1, waiting for transfers between devices, body(): g1 = lax.ppermute(gate_new, AXES, gate_pairs(1))  2.72 us
    pallas_call x1, Pallas kernels, adam(): pl.pallas_call(adam_kernel, out_shape=(gate_shape,) * 3 + (down_shape,) *...  2.54 us
  transfers between devices with their start and end apart: 15, of which 8 were waited for; matrix products, arithmetic and copies ran while one was open for 2% of the time, Pallas kernels for 9%

profile of v3, /device:TPU:16, one launch (start us, length us, event | category | flops | bytes accessed | tf_op | source)
XLA Modules:
  0.0 72.4 jit_solution(16702540413756337266)
XLA Ops:
  0.6 2.5 %shard_map.159 = (f32[24,1280]{1,0:T(8,128)}, f32[24,1280]{1,0:T(8,128)}, f32[24,1280]{1,0:T(8,128)}, f32[10,3072]{1,0:T(8,128)}, f32[10,3072]{1,0:T(8,128)}, /*index=5*/f32[10,3072]{1,0:T(8,128)}, f32[8,64,128]{2,1,0:T(8,128)}) custom-call(f32[24,1280]{1,0:T(8,128)} %gp.1, f32[24,1280]{1,0:T(8,128)} %gg.1, f32[24,1280]{1,0:T(8,128)} %gm.1, f32[24,1280]{1,0:T(8,128)} %gv.1, ...), custom_call_target="tpu_custom_call" | custom-call | tf_op jit(solution)/shard_map/pallas_call | solution.py:78
  3.2 4.8 %all-to-all-start = ((f32[8,64,128]{2,1,0:T(8,128)}), f32[8,64,128]{2,1,0:T(8,128)S(1)}, u32[]{:S(2)}, u32[]{:S(2)}) async-start(f32[8,64,128]{2,1,0:T(8,128)} %get-tuple-element.31), calls=%async_computation | async-start | bytes 524288 | tf_op jit(solution)/shard_map/all_to_all | solution.py:287
  8.0 2.5 %collective-permute-start = (f32[24,1280]{1,0:T(8,128)}, f32[24,1280]{1,0:T(8,128)S(1)}, u32[]{:S(2)}, u32[]{:S(2)}) collective-permute-start(f32[24,1280]{1,0:T(8,128)} %get-tuple-element.50), channel_id=1, source_target_pairs={{0,0},{1,64},{2,32},{3,96},{4,4},{5,68},{6,36},{7,100},{8,8},{9,72... | collective-permute-start | bytes 368648 | tf_op jit(solution)/shard_map/ppermute | solution.py:285
  10.5 5.5 %collective-permute-start.1 = (f32[24,1280]{1,0:T(8,128)}, f32[24,1280]{1,0:T(8,128)S(1)}, u32[]{:S(2)}, u32[]{:S(2)}) collective-permute-start(f32[24,1280]{1,0:T(8,128)} %get-tuple-element.50), channel_id=1, source_target_pairs={{0,64},{1,0},{2,96},{3,32},{4,68},{5,4},{6,100},{7,36},{8,72},{9,8... | collective-permute-start | bytes 368648 | tf_op jit(solution)/shard_map/ppermute | solution.py:286
  15.9 2.7 %collective-permute-done.1.g1 = f32[24,1280]{1,0:T(8,128)S(1)} collective-permute-done((f32[24,1280]{1,0:T(8,128)}, f32[24,1280]{1,0:T(8,128)S(1)}, u32[]{:S(2)}, u32[]{:S(2)}) %collective-permute-start.1) | collective-permute-done | bytes 122912 | tf_op jit(solution)/shard_map/ppermute | solution.py:286
  19.0 16.4 %all_to_all.10.maxima = f32[16,1,128]{2,1,0:T(1,128)S(1)} all-to-all(f32[16,1,128]{2,1,0:T(1,128)S(1)} %get-tuple-element.34), channel_id=1, replica_groups=mesh['yh'=2,'z'=4,'x'=4,'yl'=2,'c'=2] {'z','x'}, dimensions={0} | all-to-all | bytes 16384 | tf_op jit(solution)/shard_map/all_to_all | solution.py:289
  35.5 0.6 collective-permute-start.2
  36.2 2.1 %collective-permute-start.3 = (bf16[48,1280]{1,0:T(8,128)(2,1)S(1)}, bf16[48,1280]{1,0:T(8,128)(2,1)S(1)}, u32[]{:S(2)}, u32[]{:S(2)}) collective-permute-start(bf16[48,1280]{1,0:T(8,128)(2,1)S(1)} %get-tuple-element.35.g0), channel_id=1, source_target_pairs={{0,32},{16,48},{32,0},{48,16},{1,33},{17,49},{33,1},{49,17},{2,34}... | collective-permute-start | bytes 368648 | tf_op jit(solution)/shard_map/ppermute | solution.py:269
  38.2 1.2 %collective-permute-start.4 = (bf16[48,1280]{1,0:T(8,128)(2,1)S(1)}, bf16[48,1280]{1,0:T(8,128)(2,1)S(1)}, u32[]{:S(2)}, u32[]{:S(2)}) collective-permute-start(bf16[48,1280]{1,0:T(8,128)(2,1)S(1)} %get-tuple-element.35.g0), channel_id=1, source_target_pairs={{0,48},{16,0},{32,16},{48,32},{1,49},{17,1},{33,17},{49,33},{2,50}... | collective-permute-start | bytes 368648 | tf_op jit(solution)/shard_map/ppermute | solution.py:269
  39.4 0.6 collective-permute-start.5
  40.0 2.1 %collective-permute-start.6 = (bf16[80,768]{1,0:T(8,128)(2,1)S(1)}, bf16[80,768]{1,0:T(8,128)(2,1)S(1)}, u32[]{:S(2)}, u32[]{:S(2)}) collective-permute-start(bf16[80,768]{1,0:T(8,128)(2,1)S(1)} %get-tuple-element.36.d0), channel_id=1, source_target_pairs={{0,8},{4,12},{8,0},{12,4},{1,9},{5,13},{9,1},{13,5},{2,10},{6,14},... | collective-permute-start | bytes 368648 | tf_op jit(solution)/shard_map/ppermute | solution.py:269
  42.1 1.0 %collective-permute-done.2.g1 = bf16[48,1280]{1,0:T(8,128)(2,1)S(1)} collective-permute-done((bf16[48,1280]{1,0:T(8,128)(2,1)S(1)}, bf16[48,1280]{1,0:T(8,128)(2,1)S(1)}, u32[]{:S(2)}, u32[]{:S(2)}) %collective-permute-start.2) | collective-permute-done | bytes 122912 | tf_op jit(solution)/shard_map/ppermute | solution.py:269
  43.0 1.2 %collective-permute-start.7 = (bf16[80,768]{1,0:T(8,128)(2,1)S(1)}, bf16[80,768]{1,0:T(8,128)(2,1)S(1)}, u32[]{:S(2)}, u32[]{:S(2)}) collective-permute-start(bf16[80,768]{1,0:T(8,128)(2,1)S(1)} %get-tuple-element.36.d0), channel_id=1, source_target_pairs={{0,12},{4,0},{8,4},{12,8},{1,13},{5,1},{9,5},{13,9},{2,14},{6,2},{... | collective-permute-start | bytes 368648 | tf_op jit(solution)/shard_map/ppermute | solution.py:269
  44.2 2.6 %collective-permute-done.5.d1 = bf16[80,768]{1,0:T(8,128)(2,1)S(1)} collective-permute-done((bf16[80,768]{1,0:T(8,128)(2,1)S(1)}, bf16[80,768]{1,0:T(8,128)(2,1)S(1)}, u32[]{:S(2)}, u32[]{:S(2)}) %collective-permute-start.5) | collective-permute-done | bytes 122912 | tf_op jit(solution)/shard_map/ppermute | solution.py:269
  46.8 1.1 %collective-permute-done.7.d3 = bf16[80,768]{1,0:T(8,128)(2,1)S(1)} collective-permute-done((bf16[80,768]{1,0:T(8,128)(2,1)S(1)}, bf16[80,768]{1,0:T(8,128)(2,1)S(1)}, u32[]{:S(2)}, u32[]{:S(2)}) %collective-permute-start.7) | collective-permute-done | bytes 122912 | tf_op jit(solution)/shard_map/ppermute | solution.py:269
  48.1 0.9 %collective-permute-start.11 = (bf16[320,768]{1,0:T(8,128)(2,1)S(1)}, bf16[320,768]{1,0:T(8,128)(2,1)S(1)}, u32[]{:S(2)}, u32[]{:S(2)}) collective-permute-start(bf16[320,768]{1,0:T(8,128)(2,1)S(1)} %get-tuple-element.39.refs_0_), channel_id=1, source_target_pairs={{0,16},{16,32},{32,48},{48,0},{1,17},{17,33},{33,49},{49,1},{2,18}... | collective-permute-start | bytes 1474568 | tf_op jit(solution)/shard_map/ppermute | solution.py:269
  48.9 0.5 collective-permute-start.8
  49.5 2.5 %collective-permute-start.13 = (bf16[320,768]{1,0:T(8,128)(2,1)S(1)}, bf16[320,768]{1,0:T(8,128)(2,1)}, u32[]{:S(2)}, u32[]{:S(2)}) collective-permute-start(bf16[320,768]{1,0:T(8,128)(2,1)S(1)} %get-tuple-element.39.refs_0_), channel_id=1, source_target_pairs={{0,48},{16,0},{32,16},{48,32},{1,49},{17,1},{33,17},{49,33},{2,50}... | collective-permute-start | bytes 1474568 | tf_op jit(solution)/shard_map/ppermute | solution.py:269
  51.9 2.7 %collective-permute-start.10 = (bf16[192,1280]{1,0:T(8,128)(2,1)S(1)}, bf16[192,1280]{1,0:T(8,128)(2,1)S(1)}, u32[]{:S(2)}, u32[]{:S(2)}) collective-permute-start(bf16[192,1280]{1,0:T(8,128)(2,1)S(1)} %get-tuple-element.37.refs_0_), channel_id=1, source_target_pairs={{0,12},{4,0},{8,4},{12,8},{1,13},{5,1},{9,5},{13,9},{2,14},{6,2},{... | collective-permute-start | bytes 1474568 | tf_op jit(solution)/shard_map/ppermute | solution.py:269
  54.6 5.7 %collective-permute-done.11.refs_0_ = bf16[320,768]{1,0:T(8,128)(2,1)S(1)} collective-permute-done((bf16[320,768]{1,0:T(8,128)(2,1)S(1)}, bf16[320,768]{1,0:T(8,128)(2,1)S(1)}, u32[]{:S(2)}, u32[]{:S(2)}) %collective-permute-start.11) | collective-permute-done | bytes 491552 | tf_op jit(solution)/shard_map/ppermute | solution.py:269
  60.5 1.1 %collective-permute-done.8.refs_0_ = bf16[192,1280]{1,0:T(8,128)(2,1)S(1)} collective-permute-done((bf16[192,1280]{1,0:T(8,128)(2,1)S(1)}, bf16[192,1280]{1,0:T(8,128)(2,1)S(1)}, u32[]{:S(2)}, u32[]{:S(2)}) %collective-permute-start.8) | collective-permute-done | bytes 491552 | tf_op jit(solution)/shard_map/ppermute | solution.py:269
  61.7 0.7 copy.27
  62.4 0.7 broadcast_in_dim_reshape_squeeze.8
  63.1 0.8 %shard_map.167.refs_1_ = bf16[1280,768]{1,0:T(8,128)(2,1)} custom-call(bf16[320,768]{1,0:T(8,128)(2,1)S(1)} %get-tuple-element.39.refs_0_), custom_call_target="tpu_custom_call" | custom-call | tf_op jit(solution)/shard_map/pallas_call | solution.py:243
  63.9 0.8 %shard_map.163.refs_1_ = bf16[768,1280]{1,0:T(8,128)(2,1)} custom-call(bf16[192,1280]{1,0:T(8,128)(2,1)S(1)} %get-tuple-element.37.refs_0_), custom_call_target="tpu_custom_call" | custom-call | tf_op jit(solution)/shard_map/pallas_call | solution.py:243
  64.7 0.8 %shard_map.168.refs_1_ = bf16[1280,768]{1,0:T(8,128)(2,1)} custom-call(bf16[320,768]{1,0:T(8,128)(2,1)S(1)} %collective-permute-done.11.refs_0_, bf16[1280,768]{1,0:T(8,128)(2,1)} %shard_map.167.refs_1_), custom_call_target="tpu_custom_call", output_to_operand_aliasing={{}: (1, {})} | custom-call | tf_op jit(solution)/shard_map/pallas_call | solution.py:243
  65.5 0.8 %shard_map.164.refs_1_ = bf16[768,1280]{1,0:T(8,128)(2,1)} custom-call(bf16[192,1280]{1,0:T(8,128)(2,1)S(1)} %collective-permute-done.8.refs_0_, bf16[768,1280]{1,0:T(8,128)(2,1)} %shard_map.163.refs_1_), custom_call_target="tpu_custom_call", output_to_operand_aliasing={{}: (1, {})} | custom-call | tf_op jit(solution)/shard_map/pallas_call | solution.py:243
  66.3 1.8 %shard_map.169.refs_1_ = bf16[1280,768]{1,0:T(8,128)(2,1)} custom-call(bf16[320,768]{1,0:T(8,128)(2,1)} %collective-permute-done.13.refs_0_, bf16[1280,768]{1,0:T(8,128)(2,1)} %shard_map.168.refs_1_), custom_call_target="tpu_custom_call", output_to_operand_aliasing={{}: (1, {})} | custom-call | tf_op jit(solution)/shard_map/pallas_call | solution.py:243
  68.2 0.8 %shard_map.165.refs_1_ = bf16[768,1280]{1,0:T(8,128)(2,1)} custom-call(bf16[192,1280]{1,0:T(8,128)(2,1)S(1)} %collective-permute-done.10.refs_0_, bf16[768,1280]{1,0:T(8,128)(2,1)} %shard_map.164.refs_1_), custom_call_target="tpu_custom_call", output_to_operand_aliasing={{}: (1, {})} | custom-call | tf_op jit(solution)/shard_map/pallas_call | solution.py:243
  69.0 1.4 %collective-permute-done.12.refs_0_ = bf16[320,768]{1,0:T(8,128)(2,1)S(1)} collective-permute-done((bf16[320,768]{1,0:T(8,128)(2,1)S(1)}, bf16[320,768]{1,0:T(8,128)(2,1)S(1)}, u32[]{:S(2)}, u32[]{:S(2)}) %collective-permute-start.12) | collective-permute-done | bytes 491552 | tf_op jit(solution)/shard_map/ppermute | solution.py:269
  70.4 0.8 %shard_map.170 = bf16[1280,768]{1,0:T(8,128)(2,1)} custom-call(bf16[320,768]{1,0:T(8,128)(2,1)S(1)} %collective-permute-done.12.refs_0_, bf16[1280,768]{1,0:T(8,128)(2,1)} %shard_map.169.refs_1_), custom_call_target="tpu_custom_call", output_to_operand_aliasing={{}: (1, {})} | custom-call | tf_op jit(solution)/shard_map/pallas_call | solution.py:243
  71.6 0.8 %shard_map.166 = bf16[768,1280]{1,0:T(8,128)(2,1)} custom-call(bf16[192,1280]{1,0:T(8,128)(2,1)S(1)} %collective-permute-done.9.refs_0_, bf16[768,1280]{1,0:T(8,128)(2,1)} %shard_map.165.refs_1_), custom_call_target="tpu_custom_call", output_to_operand_aliasing={{}: (1, {})} | custom-call | tf_op jit(solution)/shard_map/pallas_call | solution.py:243
  (15 shorter events, 1.4 us)
Async XLA Ops:
  3.2 15.5 %all-to-all-start = ((f32[8,64,128]{2,1,0:T(8,128)}), f32[8,64,128]{2,1,0:T(8,128)S(1)}, u32[]{:S(2)}, u32[]{:S(2)}) async-start(f32[8,64,128]{2,1,0:T(8,128)} %get-tuple-element.31), calls=%async_computation | async-start | bytes 524288 | tf_op jit(solution)/shard_map/all_to_all | solution.py:287
  8.0 8.0 %collective-permute-start = (f32[24,1280]{1,0:T(8,128)}, f32[24,1280]{1,0:T(8,128)S(1)}, u32[]{:S(2)}, u32[]{:S(2)}) collective-permute-start(f32[24,1280]{1,0:T(8,128)} %get-tuple-element.50), channel_id=1, source_target_pairs={{0,0},{1,64},{2,32},{3,96},{4,4},{5,68},{6,36},{7,100},{8,8},{9,72... | collective-permute-start | bytes 368648 | tf_op jit(solution)/shard_map/ppermute | solution.py:285
  10.5 8.2 %collective-permute-start.1 = (f32[24,1280]{1,0:T(8,128)}, f32[24,1280]{1,0:T(8,128)S(1)}, u32[]{:S(2)}, u32[]{:S(2)}) collective-permute-start(f32[24,1280]{1,0:T(8,128)} %get-tuple-element.50), channel_id=1, source_target_pairs={{0,64},{1,0},{2,96},{3,32},{4,68},{5,4},{6,100},{7,36},{8,72},{9,8... | collective-permute-start | bytes 368648 | tf_op jit(solution)/shard_map/ppermute | solution.py:286
  35.5 7.5 %collective-permute-start.2 = (bf16[48,1280]{1,0:T(8,128)(2,1)S(1)}, bf16[48,1280]{1,0:T(8,128)(2,1)S(1)}, u32[]{:S(2)}, u32[]{:S(2)}) collective-permute-start(bf16[48,1280]{1,0:T(8,128)(2,1)S(1)} %get-tuple-element.35.g0), channel_id=1, source_target_pairs={{0,16},{16,32},{32,48},{48,0},{1,17},{17,33},{33,49},{49,1},{2,18}... | collective-permute-start | bytes 368648 | tf_op jit(solution)/shard_map/ppermute | solution.py:269
  36.2 8.0 %collective-permute-start.3 = (bf16[48,1280]{1,0:T(8,128)(2,1)S(1)}, bf16[48,1280]{1,0:T(8,128)(2,1)S(1)}, u32[]{:S(2)}, u32[]{:S(2)}) collective-permute-start(bf16[48,1280]{1,0:T(8,128)(2,1)S(1)} %get-tuple-element.35.g0), channel_id=1, source_target_pairs={{0,32},{16,48},{32,0},{48,16},{1,33},{17,49},{33,1},{49,17},{2,34}... | collective-permute-start | bytes 368648 | tf_op jit(solution)/shard_map/ppermute | solution.py:269
  38.2 6.0 %collective-permute-start.4 = (bf16[48,1280]{1,0:T(8,128)(2,1)S(1)}, bf16[48,1280]{1,0:T(8,128)(2,1)S(1)}, u32[]{:S(2)}, u32[]{:S(2)}) collective-permute-start(bf16[48,1280]{1,0:T(8,128)(2,1)S(1)} %get-tuple-element.35.g0), channel_id=1, source_target_pairs={{0,48},{16,0},{32,16},{48,32},{1,49},{17,1},{33,17},{49,33},{2,50}... | collective-permute-start | bytes 368648 | tf_op jit(solution)/shard_map/ppermute | solution.py:269
  39.4 7.4 %collective-permute-start.5 = (bf16[80,768]{1,0:T(8,128)(2,1)S(1)}, bf16[80,768]{1,0:T(8,128)(2,1)S(1)}, u32[]{:S(2)}, u32[]{:S(2)}) collective-permute-start(bf16[80,768]{1,0:T(8,128)(2,1)S(1)} %get-tuple-element.36.d0), channel_id=1, source_target_pairs={{0,4},{4,8},{8,12},{12,0},{1,5},{5,9},{9,13},{13,1},{2,6},{6,10},{... | collective-permute-start | bytes 368648 | tf_op jit(solution)/shard_map/ppermute | solution.py:269
  40.0 6.8 %collective-permute-start.6 = (bf16[80,768]{1,0:T(8,128)(2,1)S(1)}, bf16[80,768]{1,0:T(8,128)(2,1)S(1)}, u32[]{:S(2)}, u32[]{:S(2)}) collective-permute-start(bf16[80,768]{1,0:T(8,128)(2,1)S(1)} %get-tuple-element.36.d0), channel_id=1, source_target_pairs={{0,8},{4,12},{8,0},{12,4},{1,9},{5,13},{9,1},{13,5},{2,10},{6,14},... | collective-permute-start | bytes 368648 | tf_op jit(solution)/shard_map/ppermute | solution.py:269
  43.0 4.9 %collective-permute-start.7 = (bf16[80,768]{1,0:T(8,128)(2,1)S(1)}, bf16[80,768]{1,0:T(8,128)(2,1)S(1)}, u32[]{:S(2)}, u32[]{:S(2)}) collective-permute-start(bf16[80,768]{1,0:T(8,128)(2,1)S(1)} %get-tuple-element.36.d0), channel_id=1, source_target_pairs={{0,12},{4,0},{8,4},{12,8},{1,13},{5,1},{9,5},{13,9},{2,14},{6,2},{... | collective-permute-start | bytes 368648 | tf_op jit(solution)/shard_map/ppermute | solution.py:269
  48.1 12.3 %collective-permute-start.11 = (bf16[320,768]{1,0:T(8,128)(2,1)S(1)}, bf16[320,768]{1,0:T(8,128)(2,1)S(1)}, u32[]{:S(2)}, u32[]{:S(2)}) collective-permute-start(bf16[320,768]{1,0:T(8,128)(2,1)S(1)} %get-tuple-element.39.refs_0_), channel_id=1, source_target_pairs={{0,16},{16,32},{32,48},{48,0},{1,17},{17,33},{33,49},{49,1},{2,18}... | collective-permute-start | bytes 1474568 | tf_op jit(solution)/shard_map/ppermute | solution.py:269
  48.9 12.6 %collective-permute-start.8 = (bf16[192,1280]{1,0:T(8,128)(2,1)S(1)}, bf16[192,1280]{1,0:T(8,128)(2,1)S(1)}, u32[]{:S(2)}, u32[]{:S(2)}) collective-permute-start(bf16[192,1280]{1,0:T(8,128)(2,1)S(1)} %get-tuple-element.37.refs_0_), channel_id=1, source_target_pairs={{0,4},{4,8},{8,12},{12,0},{1,5},{5,9},{9,13},{13,1},{2,6},{6,10},{... | collective-permute-start | bytes 1474568 | tf_op jit(solution)/shard_map/ppermute | solution.py:269
  49.5 16.8 %collective-permute-start.13 = (bf16[320,768]{1,0:T(8,128)(2,1)S(1)}, bf16[320,768]{1,0:T(8,128)(2,1)}, u32[]{:S(2)}, u32[]{:S(2)}) collective-permute-start(bf16[320,768]{1,0:T(8,128)(2,1)S(1)} %get-tuple-element.39.refs_0_), channel_id=1, source_target_pairs={{0,48},{16,0},{32,16},{48,32},{1,49},{17,1},{33,17},{49,33},{2,50}... | collective-permute-start | bytes 1474568 | tf_op jit(solution)/shard_map/ppermute | solution.py:269
  51.9 16.2 %collective-permute-start.10 = (bf16[192,1280]{1,0:T(8,128)(2,1)S(1)}, bf16[192,1280]{1,0:T(8,128)(2,1)S(1)}, u32[]{:S(2)}, u32[]{:S(2)}) collective-permute-start(bf16[192,1280]{1,0:T(8,128)(2,1)S(1)} %get-tuple-element.37.refs_0_), channel_id=1, source_target_pairs={{0,12},{4,0},{8,4},{12,8},{1,13},{5,1},{9,5},{13,9},{2,14},{6,2},{... | collective-permute-start | bytes 1474568 | tf_op jit(solution)/shard_map/ppermute | solution.py:269
  60.3 10.0 %collective-permute-start.12 = (bf16[320,768]{1,0:T(8,128)(2,1)S(1)}, bf16[320,768]{1,0:T(8,128)(2,1)S(1)}, u32[]{:S(2)}, u32[]{:S(2)}) collective-permute-start(bf16[320,768]{1,0:T(8,128)(2,1)S(1)} %collective-permute-done.11.refs_0_), channel_id=1, source_target_pairs={{0,16},{16,32},{32,48},{48,0},{1,17},{17,33},{33,49},{49,1},{2,18}... | collective-permute-start | bytes 1474568 | tf_op jit(solution)/shard_map/ppermute | solution.py:269
  61.6 10.0 %collective-permute-start.9 = (bf16[192,1280]{1,0:T(8,128)(2,1)S(1)}, bf16[192,1280]{1,0:T(8,128)(2,1)S(1)}, u32[]{:S(2)}, u32[]{:S(2)}) collective-permute-start(bf16[192,1280]{1,0:T(8,128)(2,1)S(1)} %collective-permute-done.8.refs_0_), channel_id=1, source_target_pairs={{0,4},{4,8},{8,12},{12,0},{1,5},{5,9},{9,13},{13,1},{2,6},{6,10},{... | collective-permute-start | bytes 1474568 | tf_op jit(solution)/shard_map/ppermute | solution.py:269

commit v4 on v3

--- a/solution.py
+++ b/solution.py
@@ -58,18 +58,44 @@
     return (param_new, moment_new, second_new)
 
 
+def block_maxima(rows, first, row_count, blocks):
+    size = jnp.abs(rows)
+    below = lax.broadcasted_iota(jnp.int32, (row_count, 1), 0) < first
+    out = []
+    for part in (jnp.where(below, size, 0.0), jnp.where(below, 0.0, size)):
+        top = jnp.max(part, axis=0, keepdims=True)
+        tall = jnp.concatenate([top[:, k * BLOCK : (k + 1) * BLOCK] for k in range(blocks)], axis=0)
+        out.append(jnp.max(tall, axis=1, keepdims=True))
+    return out
+
+
+def spread(low, high, blk, count, base):
+    lane = lax.broadcasted_iota(jnp.int32, (1, LANES), 1) - base
+    row = jnp.zeros((1, LANES), jnp.float32)
+    for k in range(count):
+        row = jnp.where(lane == blk * count + k, low[k : k + 1, :], row)
+        row = jnp.where(lane == (blk + 1) * count + k, jnp.maximum(high[k : k + 1, :], row), row)
+    return row
+
+
 def adam_kernel(gp, gg, gm, gv, dp, dg, dm, dv, gpo, gmo, gvo, dpo, dmo, dvo, slots):
-    gpo[...], gmo[...], gvo[...] = adamw_step(gp[...], gg[...], gm[...], gv[...])
+    _, z, x, yl, c = [lax.axis_index(name) for name in AXES]
+    gate, gmo[...], gvo[...] = adamw_step(gp[...], gg[...], gm[...], gv[...])
     down, dmo[...], dvo[...] = adamw_step(dp[...], dg[...], dm[...], dv[...])
+    gpo[...] = gate
     dpo[...] = down
+    at = ((z % 2 * 4 + x) * 4 + yl * 2 + c) * GATE_ROWS
+    blk = at // BLOCK
+    low, high = block_maxima(gate, (blk + 1) * BLOCK - at, GATE_ROWS, GATE_BLOCKS)
+    row = spread(low, high, blk, GATE_BLOCKS, 0)
     for rank in range(4):
-        for k in range(DOWN_BLOCKS):
-            col = rank * SHARE + k * BLOCK
-            for half in range(2):
-                slots[half * 4 + rank, 8 * k : 8 * k + 8, :] = down[0:8, col : col + BLOCK]
-                slots[half * 4 + rank, 48 + 2 * k : 50 + 2 * k, :] = down[8:10, col : col + BLOCK]
         for half in range(2):
-            slots[half * 4 + rank, 60:64, :] = jnp.zeros((4, LANES), jnp.float32)
+            to = half * 4 + rank
+            for k in range(DOWN_BLOCKS):
+                col = slice(rank * SHARE + k * BLOCK, rank * SHARE + (k + 1) * BLOCK)
+                slots[to, 8 * k : 8 * k + 8, :] = down[0:8, col]
+                slots[to, 48 + 2 * k : 50 + 2 * k, :] = down[8:10, col]
+            slots[to, 60:64, :] = jnp.broadcast_to(row, (4, LANES))
 
 
 def adam(gate, down):
@@ -85,67 +111,48 @@
     )(*gate, *down)
 
 
-def block_maxima(rows, first, row_count, blocks):
-    size = jnp.abs(rows)
-    below = lax.broadcasted_iota(jnp.int32, (row_count, 1), 0) < first
-    out = []
-    for part in (jnp.where(below, size, 0.0), jnp.where(below, 0.0, size)):
-        top = jnp.max(part, axis=0, keepdims=True)
-        tall = jnp.concatenate([top[:, k * BLOCK : (k + 1) * BLOCK] for k in range(blocks)], axis=0)
-        out.append(jnp.max(tall, axis=1, keepdims=True))
-    return out
-
-
-def spread(low, high, blk, count, base):
-    lane = lax.broadcasted_iota(jnp.int32, (1, LANES), 1) - base
-    row = jnp.zeros((1, LANES), jnp.float32)
-    for k in range(count):
-        row = jnp.where(lane == blk * count + k, low[k : k + 1, :], row)
-        row = jnp.where(lane == (blk + 1) * count + k, jnp.maximum(high[k : k + 1, :], row), row)
-    return row
-
-
-def unpack_kernel(g0, g1, slots, gate, down, maxima):
-    yh, z, x = [lax.axis_index(name) for name in INST]
-    gate[pl.ds(pl.multiple_of(yh * GATE_ROWS, 8), GATE_ROWS), :] = g0[...]
-    gate[pl.ds(pl.multiple_of((1 - yh) * GATE_ROWS, 8), GATE_ROWS), :] = g1[...]
+def unpack_kernel(slots, down, maxima):
+    _, z, x, _, _ = [lax.axis_index(name) for name in AXES]
     for s in range(8):
         at = s * DOWN_ROWS
         for k in range(DOWN_BLOCKS):
             col = slice(k * BLOCK, (k + 1) * BLOCK)
             down[at : at + 8, col] = slots[s, 8 * k : 8 * k + 8, :]
             down[at + 8 : at + 10, col] = slots[s, 48 + 2 * k : 50 + 2 * k, :]
-    at = x * 96 + z // 2 * 48
-    blk = at // BLOCK
-    low, high = block_maxima(gate[...], (blk + 1) * BLOCK - at, 48, GATE_BLOCKS)
-    row = spread(low, high, 3 * (z % 2) + blk, GATE_BLOCKS, 0)
+    halves = [jnp.max(jnp.max(slots[4 * h : 4 * h + 4, 60:64, :], axis=0), axis=0, keepdims=True) for h in range(2)]
     at = z * 160 + x * 40
     blk = at // BLOCK
     for h in range(2):
         low, high = block_maxima(down[h * 40 : h * 40 + 40, :], (blk + 1) * BLOCK - at, 40, DOWN_BLOCKS)
-        row = jnp.maximum(row, spread(low, high, 5 * h + blk, DOWN_BLOCKS, DOWN_LANE))
+        halves[0] = jnp.maximum(halves[0], spread(low, high, 5 * h + blk, DOWN_BLOCKS, DOWN_LANE))
+    rows = jnp.concatenate(halves + halves, axis=0)
     for i in range(16):
-        maxima[i] = row
-
-
-def unpack(g0, g1, slots):
+        maxima[i] = rows
+
+
+def unpack(slots):
     return pl.pallas_call(
         unpack_kernel,
         out_shape=(
-            jax.ShapeDtypeStruct((48, GATE_COLS), jnp.float32),
             jax.ShapeDtypeStruct((80, SHARE), jnp.float32),
-            jax.ShapeDtypeStruct((16, 1, LANES), jnp.float32),
+            jax.ShapeDtypeStruct((16, 4, LANES), jnp.float32),
         ),
-        in_specs=[vmem()] * 3,
-        out_specs=(vmem(),) * 3,
+        in_specs=[vmem()],
+        out_specs=(vmem(),) * 2,
         compiler_params=limit(4),
-    )(g0, g1, slots)
-
-
-def quantize_kernel(gate, down, maxima, gate_out, down_out, scales):
-    yh, z, x = [lax.axis_index(name) for name in INST]
+    )(slots)
+
+
+def quantize_kernel(g0, g1, down, maxima, gate_out, down_out, scales, gate):
+    yh, z, x, yl, c = [lax.axis_index(name) for name in AXES]
+    gate[pl.ds(pl.multiple_of(yh * GATE_ROWS, 8), GATE_ROWS), :] = g0[...]
+    gate[pl.ds(pl.multiple_of((1 - yh) * GATE_ROWS, 8), GATE_ROWS), :] = g1[...]
     lane = lax.broadcasted_iota(jnp.int32, (1, LANES), 1)
-    top = jnp.max(maxima[...], axis=0) + scale_eps
+    by_core = [jnp.max(maxima[8 * i : 8 * i + 8], axis=0) for i in range(2)]
+    rows = jnp.where(c == 0, by_core[0], by_core[1])
+    gate_row = jnp.where(yl == 0, rows[0:1, :], rows[1:2, :])
+    down_row = jnp.maximum(by_core[0], by_core[1])[0:1, :]
+    top = jnp.where(lane < DOWN_LANE, gate_row, down_row) + scale_eps
     scales[...] = top
 
     def pick(at):
@@ -176,7 +183,7 @@
         down_out[:, col] = (down[:, col] / jnp.where(below, low, high)).astype(jnp.bfloat16)
 
 
-def quantize(gate, down, maxima):
+def quantize(g0, g1, down, maxima):
     return pl.pallas_call(
         quantize_kernel,
         out_shape=(
@@ -184,10 +191,11 @@
             jax.ShapeDtypeStruct((80, SHARE), jnp.bfloat16),
             jax.ShapeDtypeStruct((1, LANES), jnp.float32),
         ),
-        in_specs=[vmem()] * 3,
+        in_specs=[vmem()] * 4,
         out_specs=(vmem(),) * 3,
+        scratch_shapes=[pltpu.VMEM((48, GATE_COLS), jnp.float32)],
         compiler_params=limit(4),
-    )(gate, down, maxima)
+    )(g0, g1, down, maxima)
 
 
 def pack_kernel(g0, g1, g2, g3, d0, d1, d2, d3, gate, down, rows):
@@ -285,9 +293,9 @@
     g0 = lax.ppermute(gate_new, AXES, gate_pairs(0))
     g1 = lax.ppermute(gate_new, AXES, gate_pairs(1))
     slots = lax.all_to_all(slots, ("yh", "yl", "c"), 0, 0, tiled=True)
-    gate, down, maxima = unpack(g0, g1, slots)
+    down, maxima = unpack(slots)
     maxima = lax.all_to_all(maxima, ("z", "x"), 0, 0, tiled=True)
-    gate, down, scales = quantize(gate, down, maxima)
+    gate, down, scales = quantize(g0, g1, down, maxima)
     gate, down = pack(around(gate, "z"), around(down, "x"))
     gate_quant = place(around_by_neighbours(gate, "x"), "x")
     down_quant = place(around_by_neighbours(down, "z"), "z")

time: 72.8 us -> 68.5 us (0.941)
  the two profiles are of different devices: /device:TPU:16 before, /device:TPU:0 now
where the time goes in v4:
time: 68.5 us; the launch traced here: 68.1 us
  starting transfers between devices  33.1 us (48%)
  waiting for transfers between devices  21.5 us (31%)
  Pallas kernels  11.3 us (16%)
  local copies, waits for them, and re-layouts  1.5 us (2%)
  between operations  0.78 us (1%)
    ppermute x12, starting transfers between devices, shift(): return lax.ppermute(array, axis, [(i, (i + by) % 4) for i in range(4)])  14.3 us
    ppermute x12, waiting for transfers between devices, shift(): return lax.ppermute(array, axis, [(i, (i + by) % 4) for i in range(4)])  12.4 us
    all_to_all x1, starting transfers between devices, body(): maxima = lax.all_to_all(maxima, ('z', 'x'), 0, 0, tiled=True)  8.19 us
    all_to_all x1, waiting for transfers between devices, body(): maxima = lax.all_to_all(maxima, ('z', 'x'), 0, 0, tiled=True)  7.58 us
    pallas_call x8, Pallas kernels, place(): pl.pallas_call(functools.partial(place_kernel, axis, back), out_shape=jax...  7.45 us
    all_to_all x1, starting transfers between devices, body(): slots = lax.all_to_all(slots, ('yh', 'yl', 'c'), 0, 0, tiled=True)  4.55 us
    ppermute x1, starting transfers between devices, body(): g1 = lax.ppermute(gate_new, AXES, gate_pairs(1))  4.51 us
    pallas_call x1, Pallas kernels, adam(): pl.pallas_call(adam_kernel, out_shape=(gate_shape,) * 3 + (down_shape,) *...  2.66 us
  transfers between devices with their start and end apart: 16, of which 8 were waited for; matrix products, arithmetic and copies ran while one was open for 2% of the time, Pallas kernels for 11%

profile of v4, /device:TPU:0, one launch (start us, length us, event | category | flops | bytes accessed | tf_op | source)
XLA Modules:
  0.0 68.1 jit_solution(8917531309966844779)
XLA Ops:
  0.6 2.7 %shard_map.159 = (f32[24,1280]{1,0:T(8,128)}, f32[24,1280]{1,0:T(8,128)}, f32[24,1280]{1,0:T(8,128)}, f32[10,3072]{1,0:T(8,128)}, f32[10,3072]{1,0:T(8,128)}, /*index=5*/f32[10,3072]{1,0:T(8,128)}, f32[8,64,128]{2,1,0:T(8,128)}) custom-call(f32[24,1280]{1,0:T(8,128)} %gp.1, f32[24,1280]{1,0:T(8,128)} %gg.1, f32[24,1280]{1,0:T(8,128)} %gm.1, f32[24,1280]{1,0:T(8,128)} %gv.1, ...), custom_call_target="tpu_custom_call" | custom-call | tf_op jit(solution)/shard_map/pallas_call | solution.py:104
  3.3 4.6 %all-to-all-start = ((f32[8,64,128]{2,1,0:T(8,128)}), f32[8,64,128]{2,1,0:T(8,128)S(1)}, u32[]{:S(2)}, u32[]{:S(2)}) async-start(f32[8,64,128]{2,1,0:T(8,128)} %get-tuple-element.30), calls=%async_computation | async-start | bytes 524288 | tf_op jit(solution)/shard_map/all_to_all | solution.py:295
  7.9 1.5 %collective-permute-start = (f32[24,1280]{1,0:T(8,128)}, f32[24,1280]{1,0:T(8,128)S(1)}, u32[]{:S(2)}, u32[]{:S(2)}) collective-permute-start(f32[24,1280]{1,0:T(8,128)} %get-tuple-element.48), channel_id=1, source_target_pairs={{0,0},{1,64},{2,32},{3,96},{4,4},{5,68},{6,36},{7,100},{8,8},{9,72... | collective-permute-start | bytes 368648 | tf_op jit(solution)/shard_map/ppermute | solution.py:293
  9.4 4.5 %collective-permute-start.1 = (f32[24,1280]{1,0:T(8,128)}, f32[24,1280]{1,0:T(8,128)S(1)}, u32[]{:S(2)}, u32[]{:S(2)}) collective-permute-start(f32[24,1280]{1,0:T(8,128)} %get-tuple-element.48), channel_id=1, source_target_pairs={{0,64},{1,0},{2,96},{3,32},{4,68},{5,4},{6,100},{7,36},{8,72},{9,8... | collective-permute-start | bytes 368648 | tf_op jit(solution)/shard_map/ppermute | solution.py:294
  13.9 1.5 %all-to-all-done.slots = f32[8,64,128]{2,1,0:T(8,128)S(1)} async-done(((f32[8,64,128]{2,1,0:T(8,128)}), f32[8,64,128]{2,1,0:T(8,128)S(1)}, u32[]{:S(2)}, u32[]{:S(2)}) %all-to-all-start) | async-done | bytes 262176 | tf_op jit(solution)/shard_map/all_to_all | solution.py:295
  15.4 0.8 %shard_map.160 = (f32[80,768]{1,0:T(8,128)S(1)}, f32[16,4,128]{2,1,0:T(4,128)}) custom-call(f32[8,64,128]{2,1,0:T(8,128)S(1)} %all-to-all-done.slots), custom_call_target="tpu_custom_call" | custom-call | tf_op jit(solution)/shard_map/pallas_call | solution.py:134
  16.2 8.2 %all-to-all-start.1 = ((f32[16,4,128]{2,1,0:T(4,128)}), f32[16,4,128]{2,1,0:T(4,128)S(1)}, u32[]{:S(2)}, u32[]{:S(2)}) async-start(f32[16,4,128]{2,1,0:T(4,128)} %get-tuple-element.32), calls=%async_computation.1 | async-start | bytes 65536 | tf_op jit(solution)/shard_map/all_to_all | solution.py:297
  24.4 7.6 %all-to-all-done.1.maxima = f32[16,4,128]{2,1,0:T(4,128)S(1)} async-done(((f32[16,4,128]{2,1,0:T(4,128)}), f32[16,4,128]{2,1,0:T(4,128)S(1)}, u32[]{:S(2)}, u32[]{:S(2)}) %all-to-all-start.1) | async-done | bytes 32800 | tf_op jit(solution)/shard_map/all_to_all | solution.py:297
  32.2 0.6 collective-permute-start.2
  32.8 2.1 %collective-permute-start.3 = (bf16[48,1280]{1,0:T(8,128)(2,1)S(1)}, bf16[48,1280]{1,0:T(8,128)(2,1)S(1)}, u32[]{:S(2)}, u32[]{:S(2)}) collective-permute-start(bf16[48,1280]{1,0:T(8,128)(2,1)S(1)} %get-tuple-element.33.g0), channel_id=1, source_target_pairs={{0,32},{16,48},{32,0},{48,16},{1,33},{17,49},{33,1},{49,17},{2,34}... | collective-permute-start | bytes 368648 | tf_op jit(solution)/shard_map/ppermute | solution.py:277
  34.9 1.2 %collective-permute-start.4 = (bf16[48,1280]{1,0:T(8,128)(2,1)S(1)}, bf16[48,1280]{1,0:T(8,128)(2,1)S(1)}, u32[]{:S(2)}, u32[]{:S(2)}) collective-permute-start(bf16[48,1280]{1,0:T(8,128)(2,1)S(1)} %get-tuple-element.33.g0), channel_id=1, source_target_pairs={{0,48},{16,0},{32,16},{48,32},{1,49},{17,1},{33,17},{49,33},{2,50}... | collective-permute-start | bytes 368648 | tf_op jit(solution)/shard_map/ppermute | solution.py:277
  36.7 2.1 %collective-permute-start.6 = (bf16[80,768]{1,0:T(8,128)(2,1)S(1)}, bf16[80,768]{1,0:T(8,128)(2,1)S(1)}, u32[]{:S(2)}, u32[]{:S(2)}) collective-permute-start(bf16[80,768]{1,0:T(8,128)(2,1)S(1)} %get-tuple-element.34.d0), channel_id=1, source_target_pairs={{0,8},{4,12},{8,0},{12,4},{1,9},{5,13},{9,1},{13,5},{2,10},{6,14},... | collective-permute-start | bytes 368648 | tf_op jit(solution)/shard_map/ppermute | solution.py:277
  38.8 0.9 %collective-permute-done.2.g1 = bf16[48,1280]{1,0:T(8,128)(2,1)S(1)} collective-permute-done((bf16[48,1280]{1,0:T(8,128)(2,1)S(1)}, bf16[48,1280]{1,0:T(8,128)(2,1)S(1)}, u32[]{:S(2)}, u32[]{:S(2)}) %collective-permute-start.2) | collective-permute-done | bytes 122912 | tf_op jit(solution)/shard_map/ppermute | solution.py:277
  39.7 1.2 %collective-permute-start.7 = (bf16[80,768]{1,0:T(8,128)(2,1)S(1)}, bf16[80,768]{1,0:T(8,128)(2,1)S(1)}, u32[]{:S(2)}, u32[]{:S(2)}) collective-permute-start(bf16[80,768]{1,0:T(8,128)(2,1)S(1)} %get-tuple-element.34.d0), channel_id=1, source_target_pairs={{0,12},{4,0},{8,4},{12,8},{1,13},{5,1},{9,5},{13,9},{2,14},{6,2},{... | collective-permute-start | bytes 368648 | tf_op jit(solution)/shard_map/ppermute | solution.py:277
  40.9 2.6 %collective-permute-done.5.d1 = bf16[80,768]{1,0:T(8,128)(2,1)S(1)} collective-permute-done((bf16[80,768]{1,0:T(8,128)(2,1)S(1)}, bf16[80,768]{1,0:T(8,128)(2,1)S(1)}, u32[]{:S(2)}, u32[]{:S(2)}) %collective-permute-start.5) | collective-permute-done | bytes 122912 | tf_op jit(solution)/shard_map/ppermute | solution.py:277
  43.5 1.1 %collective-permute-done.7.d3 = bf16[80,768]{1,0:T(8,128)(2,1)S(1)} collective-permute-done((bf16[80,768]{1,0:T(8,128)(2,1)S(1)}, bf16[80,768]{1,0:T(8,128)(2,1)S(1)}, u32[]{:S(2)}, u32[]{:S(2)}) %collective-permute-start.7) | collective-permute-done | bytes 122912 | tf_op jit(solution)/shard_map/ppermute | solution.py:277
  44.8 0.7 %collective-permute-start.11 = (bf16[320,768]{1,0:T(8,128)(2,1)S(1)}, bf16[320,768]{1,0:T(8,128)(2,1)S(1)}, u32[]{:S(2)}, u32[]{:S(2)}) collective-permute-start(bf16[320,768]{1,0:T(8,128)(2,1)S(1)} %get-tuple-element.37.refs_0_), channel_id=1, source_target_pairs={{0,16},{16,32},{32,48},{48,0},{1,17},{17,33},{33,49},{49,1},{2,18}... | collective-permute-start | bytes 1474568 | tf_op jit(solution)/shard_map/ppermute | solution.py:277
  45.5 0.7 %collective-permute-start.8 = (bf16[192,1280]{1,0:T(8,128)(2,1)S(1)}, bf16[192,1280]{1,0:T(8,128)(2,1)S(1)}, u32[]{:S(2)}, u32[]{:S(2)}) collective-permute-start(bf16[192,1280]{1,0:T(8,128)(2,1)S(1)} %get-tuple-element.35.refs_0_), channel_id=1, source_target_pairs={{0,4},{4,8},{8,12},{12,0},{1,5},{5,9},{9,13},{13,1},{2,6},{6,10},{... | collective-permute-start | bytes 1474568 | tf_op jit(solution)/shard_map/ppermute | solution.py:277
  46.2 2.5 %collective-permute-start.13 = (bf16[320,768]{1,0:T(8,128)(2,1)S(1)}, bf16[320,768]{1,0:T(8,128)(2,1)}, u32[]{:S(2)}, u32[]{:S(2)}) collective-permute-start(bf16[320,768]{1,0:T(8,128)(2,1)S(1)} %get-tuple-element.37.refs_0_), channel_id=1, source_target_pairs={{0,48},{16,0},{32,16},{48,32},{1,49},{17,1},{33,17},{49,33},{2,50}... | collective-permute-start | bytes 1474568 | tf_op jit(solution)/shard_map/ppermute | solution.py:277
  48.6 2.7 %collective-permute-start.10 = (bf16[192,1280]{1,0:T(8,128)(2,1)S(1)}, bf16[192,1280]{1,0:T(8,128)(2,1)S(1)}, u32[]{:S(2)}, u32[]{:S(2)}) collective-permute-start(bf16[192,1280]{1,0:T(8,128)(2,1)S(1)} %get-tuple-element.35.refs_0_), channel_id=1, source_target_pairs={{0,12},{4,0},{8,4},{12,8},{1,13},{5,1},{9,5},{13,9},{2,14},{6,2},{... | collective-permute-start | bytes 1474568 | tf_op jit(solution)/shard_map/ppermute | solution.py:277
  51.3 5.2 %collective-permute-done.11.refs_0_ = bf16[320,768]{1,0:T(8,128)(2,1)S(1)} collective-permute-done((bf16[320,768]{1,0:T(8,128)(2,1)S(1)}, bf16[320,768]{1,0:T(8,128)(2,1)S(1)}, u32[]{:S(2)}, u32[]{:S(2)}) %collective-permute-start.11) | collective-permute-done | bytes 491552 | tf_op jit(solution)/shard_map/ppermute | solution.py:277
  57.2 0.7 copy.27
  57.8 0.7 broadcast_in_dim_reshape_squeeze.8
  58.5 0.8 %shard_map.167.refs_1_ = bf16[1280,768]{1,0:T(8,128)(2,1)} custom-call(bf16[320,768]{1,0:T(8,128)(2,1)S(1)} %get-tuple-element.37.refs_0_), custom_call_target="tpu_custom_call" | custom-call | tf_op jit(solution)/shard_map/pallas_call | solution.py:251
  59.3 0.8 %shard_map.163.refs_1_ = bf16[768,1280]{1,0:T(8,128)(2,1)} custom-call(bf16[192,1280]{1,0:T(8,128)(2,1)S(1)} %get-tuple-element.35.refs_0_), custom_call_target="tpu_custom_call" | custom-call | tf_op jit(solution)/shard_map/pallas_call | solution.py:251
  60.1 0.8 %shard_map.168.refs_1_ = bf16[1280,768]{1,0:T(8,128)(2,1)} custom-call(bf16[320,768]{1,0:T(8,128)(2,1)S(1)} %collective-permute-done.11.refs_0_, bf16[1280,768]{1,0:T(8,128)(2,1)} %shard_map.167.refs_1_), custom_call_target="tpu_custom_call", output_to_operand_aliasing={{}: (1, {})} | custom-call | tf_op jit(solution)/shard_map/pallas_call | solution.py:251
  60.9 0.8 %shard_map.164.refs_1_ = bf16[768,1280]{1,0:T(8,128)(2,1)} custom-call(bf16[192,1280]{1,0:T(8,128)(2,1)S(1)} %collective-permute-done.8.refs_0_, bf16[768,1280]{1,0:T(8,128)(2,1)} %shard_map.163.refs_1_), custom_call_target="tpu_custom_call", output_to_operand_aliasing={{}: (1, {})} | custom-call | tf_op jit(solution)/shard_map/pallas_call | solution.py:251
  61.8 1.8 %shard_map.169.refs_1_ = bf16[1280,768]{1,0:T(8,128)(2,1)} custom-call(bf16[320,768]{1,0:T(8,128)(2,1)} %collective-permute-done.13.refs_0_, bf16[1280,768]{1,0:T(8,128)(2,1)} %shard_map.168.refs_1_), custom_call_target="tpu_custom_call", output_to_operand_aliasing={{}: (1, {})} | custom-call | tf_op jit(solution)/shard_map/pallas_call | solution.py:251
  63.6 0.8 %shard_map.165.refs_1_ = bf16[768,1280]{1,0:T(8,128)(2,1)} custom-call(bf16[192,1280]{1,0:T(8,128)(2,1)S(1)} %collective-permute-done.10.refs_0_, bf16[768,1280]{1,0:T(8,128)(2,1)} %shard_map.164.refs_1_), custom_call_target="tpu_custom_call", output_to_operand_aliasing={{}: (1, {})} | custom-call | tf_op jit(solution)/shard_map/pallas_call | solution.py:251
  64.4 2.1 %collective-permute-done.12.refs_0_ = bf16[320,768]{1,0:T(8,128)(2,1)S(1)} collective-permute-done((bf16[320,768]{1,0:T(8,128)(2,1)S(1)}, bf16[320,768]{1,0:T(8,128)(2,1)S(1)}, u32[]{:S(2)}, u32[]{:S(2)}) %collective-permute-start.12) | collective-permute-done | bytes 491552 | tf_op jit(solution)/shard_map/ppermute | solution.py:277
  66.5 0.8 %shard_map.170 = bf16[1280,768]{1,0:T(8,128)(2,1)} custom-call(bf16[320,768]{1,0:T(8,128)(2,1)S(1)} %collective-permute-done.12.refs_0_, bf16[1280,768]{1,0:T(8,128)(2,1)} %shard_map.169.refs_1_), custom_call_target="tpu_custom_call", output_to_operand_aliasing={{}: (1, {})} | custom-call | tf_op jit(solution)/shard_map/pallas_call | solution.py:251
  67.3 0.8 %shard_map.166 = bf16[768,1280]{1,0:T(8,128)(2,1)} custom-call(bf16[192,1280]{1,0:T(8,128)(2,1)S(1)} %collective-permute-done.9.refs_0_, bf16[768,1280]{1,0:T(8,128)(2,1)} %shard_map.165.refs_1_), custom_call_target="tpu_custom_call", output_to_operand_aliasing={{}: (1, {})} | custom-call | tf_op jit(solution)/shard_map/pallas_call | solution.py:251
  (16 shorter events, 1.7 us)
Async XLA Ops:
  3.3 12.1 %all-to-all-start = ((f32[8,64,128]{2,1,0:T(8,128)}), f32[8,64,128]{2,1,0:T(8,128)S(1)}, u32[]{:S(2)}, u32[]{:S(2)}) async-start(f32[8,64,128]{2,1,0:T(8,128)} %get-tuple-element.30), calls=%async_computation | async-start | bytes 524288 | tf_op jit(solution)/shard_map/all_to_all | solution.py:295
  7.9 16.6 %collective-permute-start = (f32[24,1280]{1,0:T(8,128)}, f32[24,1280]{1,0:T(8,128)S(1)}, u32[]{:S(2)}, u32[]{:S(2)}) collective-permute-start(f32[24,1280]{1,0:T(8,128)} %get-tuple-element.48), channel_id=1, source_target_pairs={{0,0},{1,64},{2,32},{3,96},{4,4},{5,68},{6,36},{7,100},{8,8},{9,72... | collective-permute-start | bytes 368648 | tf_op jit(solution)/shard_map/ppermute | solution.py:293
  9.4 15.0 %collective-permute-start.1 = (f32[24,1280]{1,0:T(8,128)}, f32[24,1280]{1,0:T(8,128)S(1)}, u32[]{:S(2)}, u32[]{:S(2)}) collective-permute-start(f32[24,1280]{1,0:T(8,128)} %get-tuple-element.48), channel_id=1, source_target_pairs={{0,64},{1,0},{2,96},{3,32},{4,68},{5,4},{6,100},{7,36},{8,72},{9,8... | collective-permute-start | bytes 368648 | tf_op jit(solution)/shard_map/ppermute | solution.py:294
  16.2 15.8 %all-to-all-start.1 = ((f32[16,4,128]{2,1,0:T(4,128)}), f32[16,4,128]{2,1,0:T(4,128)S(1)}, u32[]{:S(2)}, u32[]{:S(2)}) async-start(f32[16,4,128]{2,1,0:T(4,128)} %get-tuple-element.32), calls=%async_computation.1 | async-start | bytes 65536 | tf_op jit(solution)/shard_map/all_to_all | solution.py:297
  32.2 7.5 %collective-permute-start.2 = (bf16[48,1280]{1,0:T(8,128)(2,1)S(1)}, bf16[48,1280]{1,0:T(8,128)(2,1)S(1)}, u32[]{:S(2)}, u32[]{:S(2)}) collective-permute-start(bf16[48,1280]{1,0:T(8,128)(2,1)S(1)} %get-tuple-element.33.g0), channel_id=1, source_target_pairs={{0,16},{16,32},{32,48},{48,0},{1,17},{17,33},{33,49},{49,1},{2,18}... | collective-permute-start | bytes 368648 | tf_op jit(solution)/shard_map/ppermute | solution.py:277
  32.8 8.0 %collective-permute-start.3 = (bf16[48,1280]{1,0:T(8,128)(2,1)S(1)}, bf16[48,1280]{1,0:T(8,128)(2,1)S(1)}, u32[]{:S(2)}, u32[]{:S(2)}) collective-permute-start(bf16[48,1280]{1,0:T(8,128)(2,1)S(1)} %get-tuple-element.33.g0), channel_id=1, source_target_pairs={{0,32},{16,48},{32,0},{48,16},{1,33},{17,49},{33,1},{49,17},{2,34}... | collective-permute-start | bytes 368648 | tf_op jit(solution)/shard_map/ppermute | solution.py:277
  34.9 6.0 %collective-permute-start.4 = (bf16[48,1280]{1,0:T(8,128)(2,1)S(1)}, bf16[48,1280]{1,0:T(8,128)(2,1)S(1)}, u32[]{:S(2)}, u32[]{:S(2)}) collective-permute-start(bf16[48,1280]{1,0:T(8,128)(2,1)S(1)} %get-tuple-element.33.g0), channel_id=1, source_target_pairs={{0,48},{16,0},{32,16},{48,32},{1,49},{17,1},{33,17},{49,33},{2,50}... | collective-permute-start | bytes 368648 | tf_op jit(solution)/shard_map/ppermute | solution.py:277
  36.1 7.4 %collective-permute-start.5 = (bf16[80,768]{1,0:T(8,128)(2,1)S(1)}, bf16[80,768]{1,0:T(8,128)(2,1)S(1)}, u32[]{:S(2)}, u32[]{:S(2)}) collective-permute-start(bf16[80,768]{1,0:T(8,128)(2,1)S(1)} %get-tuple-element.34.d0), channel_id=1, source_target_pairs={{0,4},{4,8},{8,12},{12,0},{1,5},{5,9},{9,13},{13,1},{2,6},{6,10},{... | collective-permute-start | bytes 368648 | tf_op jit(solution)/shard_map/ppermute | solution.py:277
  36.7 6.8 %collective-permute-start.6 = (bf16[80,768]{1,0:T(8,128)(2,1)S(1)}, bf16[80,768]{1,0:T(8,128)(2,1)S(1)}, u32[]{:S(2)}, u32[]{:S(2)}) collective-permute-start(bf16[80,768]{1,0:T(8,128)(2,1)S(1)} %get-tuple-element.34.d0), channel_id=1, source_target_pairs={{0,8},{4,12},{8,0},{12,4},{1,9},{5,13},{9,1},{13,5},{2,10},{6,14},... | collective-permute-start | bytes 368648 | tf_op jit(solution)/shard_map/ppermute | solution.py:277
  39.7 4.9 %collective-permute-start.7 = (bf16[80,768]{1,0:T(8,128)(2,1)S(1)}, bf16[80,768]{1,0:T(8,128)(2,1)S(1)}, u32[]{:S(2)}, u32[]{:S(2)}) collective-permute-start(bf16[80,768]{1,0:T(8,128)(2,1)S(1)} %get-tuple-element.34.d0), channel_id=1, source_target_pairs={{0,12},{4,0},{8,4},{12,8},{1,13},{5,1},{9,5},{13,9},{2,14},{6,2},{... | collective-permute-start | bytes 368648 | tf_op jit(solution)/shard_map/ppermute | solution.py:277
  44.8 11.7 %collective-permute-start.11 = (bf16[320,768]{1,0:T(8,128)(2,1)S(1)}, bf16[320,768]{1,0:T(8,128)(2,1)S(1)}, u32[]{:S(2)}, u32[]{:S(2)}) collective-permute-start(bf16[320,768]{1,0:T(8,128)(2,1)S(1)} %get-tuple-element.37.refs_0_), channel_id=1, source_target_pairs={{0,16},{16,32},{32,48},{48,0},{1,17},{17,33},{33,49},{49,1},{2,18}... | collective-permute-start | bytes 1474568 | tf_op jit(solution)/shard_map/ppermute | solution.py:277
  45.5 11.5 %collective-permute-start.8 = (bf16[192,1280]{1,0:T(8,128)(2,1)S(1)}, bf16[192,1280]{1,0:T(8,128)(2,1)S(1)}, u32[]{:S(2)}, u32[]{:S(2)}) collective-permute-start(bf16[192,1280]{1,0:T(8,128)(2,1)S(1)} %get-tuple-element.35.refs_0_), channel_id=1, source_target_pairs={{0,4},{4,8},{8,12},{12,0},{1,5},{5,9},{9,13},{13,1},{2,6},{6,10},{... | collective-permute-start | bytes 1474568 | tf_op jit(solution)/shard_map/ppermute | solution.py:277
  46.2 15.6 %collective-permute-start.13 = (bf16[320,768]{1,0:T(8,128)(2,1)S(1)}, bf16[320,768]{1,0:T(8,128)(2,1)}, u32[]{:S(2)}, u32[]{:S(2)}) collective-permute-start(bf16[320,768]{1,0:T(8,128)(2,1)S(1)} %get-tuple-element.37.refs_0_), channel_id=1, source_target_pairs={{0,48},{16,0},{32,16},{48,32},{1,49},{17,1},{33,17},{49,33},{2,50}... | collective-permute-start | bytes 1474568 | tf_op jit(solution)/shard_map/ppermute | solution.py:277
  48.6 15.0 %collective-permute-start.10 = (bf16[192,1280]{1,0:T(8,128)(2,1)S(1)}, bf16[192,1280]{1,0:T(8,128)(2,1)S(1)}, u32[]{:S(2)}, u32[]{:S(2)}) collective-permute-start(bf16[192,1280]{1,0:T(8,128)(2,1)S(1)} %get-tuple-element.35.refs_0_), channel_id=1, source_target_pairs={{0,12},{4,0},{8,4},{12,8},{1,13},{5,1},{9,5},{13,9},{2,14},{6,2},{... | collective-permute-start | bytes 1474568 | tf_op jit(solution)/shard_map/ppermute | solution.py:277
  56.5 10.0 %collective-permute-start.12 = (bf16[320,768]{1,0:T(8,128)(2,1)S(1)}, bf16[320,768]{1,0:T(8,128)(2,1)S(1)}, u32[]{:S(2)}, u32[]{:S(2)}) collective-permute-start(bf16[320,768]{1,0:T(8,128)(2,1)S(1)} %collective-permute-done.11.refs_0_), channel_id=1, source_target_pairs={{0,16},{16,32},{32,48},{48,0},{1,17},{17,33},{33,49},{49,1},{2,18}... | collective-permute-start | bytes 1474568 | tf_op jit(solution)/shard_map/ppermute | solution.py:277
  57.0 10.3 %collective-permute-start.9 = (bf16[192,1280]{1,0:T(8,128)(2,1)S(1)}, bf16[192,1280]{1,0:T(8,128)(2,1)S(1)}, u32[]{:S(2)}, u32[]{:S(2)}) collective-permute-start(bf16[192,1280]{1,0:T(8,128)(2,1)S(1)} %collective-permute-done.8.refs_0_), channel_id=1, source_target_pairs={{0,4},{4,8},{8,12},{12,0},{1,5},{5,9},{9,13},{13,1},{2,6},{6,10},{... | collective-permute-start | bytes 1474568 | tf_op jit(solution)/shard_map/ppermute | solution.py:277

commit v5 on v4

--- a/solution.py
+++ b/solution.py
@@ -70,12 +70,10 @@
 
 
 def spread(low, high, blk, count, base):
-    lane = lax.broadcasted_iota(jnp.int32, (1, LANES), 1) - base
-    row = jnp.zeros((1, LANES), jnp.float32)
-    for k in range(count):
-        row = jnp.where(lane == blk * count + k, low[k : k + 1, :], row)
-        row = jnp.where(lane == (blk + 1) * count + k, jnp.maximum(high[k : k + 1, :], row), row)
-    return row
+    lane = lax.broadcasted_iota(jnp.int32, (count, LANES), 1) - base
+    first = blk * count + lax.broadcasted_iota(jnp.int32, (count, LANES), 0)
+    both = jnp.where(lane == first, low, 0.0) + jnp.where(lane == first + count, high, 0.0)
+    return jnp.max(both, axis=0, keepdims=True)
 
 
 def adam_kernel(gp, gg, gm, gv, dp, dg, dm, dv, gpo, gmo, gvo, dpo, dmo, dvo, slots):
@@ -125,7 +123,7 @@
     for h in range(2):
         low, high = block_maxima(down[h * 40 : h * 40 + 40, :], (blk + 1) * BLOCK - at, 40, DOWN_BLOCKS)
         halves[0] = jnp.maximum(halves[0], spread(low, high, 5 * h + blk, DOWN_BLOCKS, DOWN_LANE))
-    rows = jnp.concatenate(halves + halves, axis=0)
+    rows = jnp.concatenate(halves, axis=0)
     for i in range(16):
         maxima[i] = rows
 
@@ -135,7 +133,7 @@
         unpack_kernel,
         out_shape=(
             jax.ShapeDtypeStruct((80, SHARE), jnp.float32),
-            jax.ShapeDtypeStruct((16, 4, LANES), jnp.float32),
+            jax.ShapeDtypeStruct((16, 2, LANES), jnp.float32),
         ),
         in_specs=[vmem()],
         out_specs=(vmem(),) * 2,
@@ -277,13 +275,14 @@
     return lax.ppermute(array, axis, [(i, (i + by) % 4) for i in range(4)])
 
 
-def around(array, axis):
-    return [array] + [shift(array, axis, by) for by in (1, 2, 3)]
-
-
-def around_by_neighbours(array, axis):
-    back = shift(array, axis, 1)
-    return [array, back, shift(back, axis, 1), shift(array, axis, 3)]
+def around(array, axis, order):
+    moved = {by: shift(array, axis, by) for by in order}
+    return [array] + [moved[by] for by in (1, 2, 3)]
+
+
+def around_by_neighbours(array, axis, way):
+    near = {by: shift(array, axis, by) for by in (way, 4 - way)}
+    return [array, near[1], shift(near[way], axis, way), near[3]]
 
 
 def body(gate_param, gate_grad, gate_m, gate_v, down_param, down_grad, down_m, down_v):
@@ -296,9 +295,9 @@
     down, maxima = unpack(slots)
     maxima = lax.all_to_all(maxima, ("z", "x"), 0, 0, tiled=True)
     gate, down, scales = quantize(g0, g1, down, maxima)
-    gate, down = pack(around(gate, "z"), around(down, "x"))
-    gate_quant = place(around_by_neighbours(gate, "x"), "x")
-    down_quant = place(around_by_neighbours(down, "z"), "z")
+    gate, down = pack(around(gate, "z", (1, 2, 3)), around(down, "x", (2, 1, 3)))
+    gate_quant = place(around_by_neighbours(gate, "x", 1), "x")
+    down_quant = place(around_by_neighbours(down, "z", 3), "z")
     gate_scale = scales[0, :60].reshape(6, 10)
     down_scale = scales[0, DOWN_LANE : DOWN_LANE + 60].reshape(10, 6)
     return (

time: 68.5 us -> 68.5 us (level)
  no operation moved by 1% of the time
where the time goes in v5:
time: 68.5 us; the launch traced here: 68.1 us
  starting transfers between devices  33.1 us (48%)
  waiting for transfers between devices  21.5 us (31%)
  Pallas kernels  11.3 us (16%)
  local copies, waits for them, and re-layouts  1.5 us (2%)
  between operations  0.77 us (1%)
    ppermute x12, starting transfers between devices, shift(): return lax.ppermute(array, axis, [(i, (i + by) % 4) for i in range(4)])  14.3 us
    ppermute x12, waiting for transfers between devices, shift(): return lax.ppermute(array, axis, [(i, (i + by) % 4) for i in range(4)])  12.5 us
    all_to_all x1, starting transfers between devices, body(): maxima = lax.all_to_all(maxima, ('z', 'x'), 0, 0, tiled=True)  8.19 us
    all_to_all x1, waiting for transfers between devices, body(): maxima = lax.all_to_all(maxima, ('z', 'x'), 0, 0, tiled=True)  7.56 us
    pallas_call x8, Pallas kernels, place(): pl.pallas_call(functools.partial(place_kernel, axis, back), out_shape=jax...  7.45 us
    all_to_all x1, starting transfers between devices, body(): slots = lax.all_to_all(slots, ('yh', 'yl', 'c'), 0, 0, tiled=True)  4.55 us
    ppermute x1, starting transfers between devices, body(): g1 = lax.ppermute(gate_new, AXES, gate_pairs(1))  4.51 us
    pallas_call x1, Pallas kernels, adam(): pl.pallas_call(adam_kernel, out_shape=(gate_shape,) * 3 + (down_shape,) *...  2.66 us
  transfers between devices with their start and end apart: 16, of which 8 were waited for; matrix products, arithmetic and copies ran while one was open for 2% of the time, Pallas kernels for 11%

profile of v5, /device:TPU:0, one launch (start us, length us, event | category | flops | bytes accessed | tf_op | source)
XLA Modules:
  0.0 68.1 jit_solution(16559454358306751440)
XLA Ops:
  0.6 2.7 %shard_map.159 = (f32[24,1280]{1,0:T(8,128)}, f32[24,1280]{1,0:T(8,128)}, f32[24,1280]{1,0:T(8,128)}, f32[10,3072]{1,0:T(8,128)}, f32[10,3072]{1,0:T(8,128)}, /*index=5*/f32[10,3072]{1,0:T(8,128)}, f32[8,64,128]{2,1,0:T(8,128)}) custom-call(f32[24,1280]{1,0:T(8,128)} %gp.1, f32[24,1280]{1,0:T(8,128)} %gg.1, f32[24,1280]{1,0:T(8,128)} %gm.1, f32[24,1280]{1,0:T(8,128)} %gv.1, ...), custom_call_target="tpu_custom_call" | custom-call | tf_op jit(solution)/shard_map/pallas_call | solution.py:102
  3.3 4.6 %all-to-all-start = ((f32[8,64,128]{2,1,0:T(8,128)}), f32[8,64,128]{2,1,0:T(8,128)S(1)}, u32[]{:S(2)}, u32[]{:S(2)}) async-start(f32[8,64,128]{2,1,0:T(8,128)} %get-tuple-element.30), calls=%async_computation | async-start | bytes 524288 | tf_op jit(solution)/shard_map/all_to_all | solution.py:294
  7.9 1.5 %collective-permute-start = (f32[24,1280]{1,0:T(8,128)}, f32[24,1280]{1,0:T(8,128)S(1)}, u32[]{:S(2)}, u32[]{:S(2)}) collective-permute-start(f32[24,1280]{1,0:T(8,128)} %get-tuple-element.48), channel_id=1, source_target_pairs={{0,0},{1,64},{2,32},{3,96},{4,4},{5,68},{6,36},{7,100},{8,8},{9,72... | collective-permute-start | bytes 368648 | tf_op jit(solution)/shard_map/ppermute | solution.py:292
  9.4 4.5 %collective-permute-start.1 = (f32[24,1280]{1,0:T(8,128)}, f32[24,1280]{1,0:T(8,128)S(1)}, u32[]{:S(2)}, u32[]{:S(2)}) collective-permute-start(f32[24,1280]{1,0:T(8,128)} %get-tuple-element.48), channel_id=1, source_target_pairs={{0,64},{1,0},{2,96},{3,32},{4,68},{5,4},{6,100},{7,36},{8,72},{9,8... | collective-permute-start | bytes 368648 | tf_op jit(solution)/shard_map/ppermute | solution.py:293
  13.9 1.5 %all-to-all-done.slots = f32[8,64,128]{2,1,0:T(8,128)S(1)} async-done(((f32[8,64,128]{2,1,0:T(8,128)}), f32[8,64,128]{2,1,0:T(8,128)S(1)}, u32[]{:S(2)}, u32[]{:S(2)}) %all-to-all-start) | async-done | bytes 262176 | tf_op jit(solution)/shard_map/all_to_all | solution.py:294
  15.4 0.8 %shard_map.160 = (f32[80,768]{1,0:T(8,128)S(1)}, f32[16,2,128]{2,1,0:T(2,128)}) custom-call(f32[8,64,128]{2,1,0:T(8,128)S(1)} %all-to-all-done.slots), custom_call_target="tpu_custom_call" | custom-call | tf_op jit(solution)/shard_map/pallas_call | solution.py:132
  16.2 8.2 %all-to-all-start.1 = ((f32[16,2,128]{2,1,0:T(2,128)}), f32[16,2,128]{2,1,0:T(2,128)S(1)}, u32[]{:S(2)}, u32[]{:S(2)}) async-start(f32[16,2,128]{2,1,0:T(2,128)} %get-tuple-element.32), calls=%async_computation.1 | async-start | bytes 32768 | tf_op jit(solution)/shard_map/all_to_all | solution.py:296
  24.4 7.6 %all-to-all-done.1.maxima = f32[16,2,128]{2,1,0:T(2,128)S(1)} async-done(((f32[16,2,128]{2,1,0:T(2,128)}), f32[16,2,128]{2,1,0:T(2,128)S(1)}, u32[]{:S(2)}, u32[]{:S(2)}) %all-to-all-start.1) | async-done | bytes 16416 | tf_op jit(solution)/shard_map/all_to_all | solution.py:296
  32.8 2.1 %collective-permute-start.3 = (bf16[48,1280]{1,0:T(8,128)(2,1)S(1)}, bf16[48,1280]{1,0:T(8,128)(2,1)S(1)}, u32[]{:S(2)}, u32[]{:S(2)}) collective-permute-start(bf16[48,1280]{1,0:T(8,128)(2,1)S(1)} %get-tuple-element.33.g0), channel_id=1, source_target_pairs={{0,32},{16,48},{32,0},{48,16},{1,33},{17,49},{33,1},{49,17},{2,34}... | collective-permute-start | bytes 368648 | tf_op jit(solution)/shard_map/ppermute | solution.py:275
  34.9 1.2 %collective-permute-start.4 = (bf16[48,1280]{1,0:T(8,128)(2,1)S(1)}, bf16[48,1280]{1,0:T(8,128)(2,1)S(1)}, u32[]{:S(2)}, u32[]{:S(2)}) collective-permute-start(bf16[48,1280]{1,0:T(8,128)(2,1)S(1)} %get-tuple-element.33.g0), channel_id=1, source_target_pairs={{0,48},{16,0},{32,16},{48,32},{1,49},{17,1},{33,17},{49,33},{2,50}... | collective-permute-start | bytes 368648 | tf_op jit(solution)/shard_map/ppermute | solution.py:275
  36.6 2.1 %collective-permute-start.6 = (bf16[80,768]{1,0:T(8,128)(2,1)S(1)}, bf16[80,768]{1,0:T(8,128)(2,1)S(1)}, u32[]{:S(2)}, u32[]{:S(2)}) collective-permute-start(bf16[80,768]{1,0:T(8,128)(2,1)S(1)} %get-tuple-element.34.d0), channel_id=1, source_target_pairs={{0,8},{4,12},{8,0},{12,4},{1,9},{5,13},{9,1},{13,5},{2,10},{6,14},... | collective-permute-start | bytes 368648 | tf_op jit(solution)/shard_map/ppermute | solution.py:275
  38.7 0.9 %collective-permute-done.2.g1 = bf16[48,1280]{1,0:T(8,128)(2,1)S(1)} collective-permute-done((bf16[48,1280]{1,0:T(8,128)(2,1)S(1)}, bf16[48,1280]{1,0:T(8,128)(2,1)S(1)}, u32[]{:S(2)}, u32[]{:S(2)}) %collective-permute-start.2) | collective-permute-done | bytes 122912 | tf_op jit(solution)/shard_map/ppermute | solution.py:275
  39.7 1.2 %collective-permute-start.7 = (bf16[80,768]{1,0:T(8,128)(2,1)S(1)}, bf16[80,768]{1,0:T(8,128)(2,1)S(1)}, u32[]{:S(2)}, u32[]{:S(2)}) collective-permute-start(bf16[80,768]{1,0:T(8,128)(2,1)S(1)} %get-tuple-element.34.d0), channel_id=1, source_target_pairs={{0,12},{4,0},{8,4},{12,8},{1,13},{5,1},{9,5},{13,9},{2,14},{6,2},{... | collective-permute-start | bytes 368648 | tf_op jit(solution)/shard_map/ppermute | solution.py:275
  40.8 2.6 %collective-permute-done.5.d1 = bf16[80,768]{1,0:T(8,128)(2,1)S(1)} collective-permute-done((bf16[80,768]{1,0:T(8,128)(2,1)S(1)}, bf16[80,768]{1,0:T(8,128)(2,1)S(1)}, u32[]{:S(2)}, u32[]{:S(2)}) %collective-permute-start.5) | collective-permute-done | bytes 122912 | tf_op jit(solution)/shard_map/ppermute | solution.py:275
  43.5 1.1 %collective-permute-done.7.d3 = bf16[80,768]{1,0:T(8,128)(2,1)S(1)} collective-permute-done((bf16[80,768]{1,0:T(8,128)(2,1)S(1)}, bf16[80,768]{1,0:T(8,128)(2,1)S(1)}, u32[]{:S(2)}, u32[]{:S(2)}) %collective-permute-start.7) | collective-permute-done | bytes 122912 | tf_op jit(solution)/shard_map/ppermute | solution.py:275
  44.7 0.7 %collective-permute-start.11 = (bf16[320,768]{1,0:T(8,128)(2,1)S(1)}, bf16[320,768]{1,0:T(8,128)(2,1)S(1)}, u32[]{:S(2)}, u32[]{:S(2)}) collective-permute-start(bf16[320,768]{1,0:T(8,128)(2,1)S(1)} %get-tuple-element.37.refs_0_), channel_id=1, source_target_pairs={{0,48},{16,0},{32,16},{48,32},{1,49},{17,1},{33,17},{49,33},{2,50}... | collective-permute-start | bytes 1474568 | tf_op jit(solution)/shard_map/ppermute | solution.py:275
  45.4 0.7 %collective-permute-start.8 = (bf16[192,1280]{1,0:T(8,128)(2,1)S(1)}, bf16[192,1280]{1,0:T(8,128)(2,1)S(1)}, u32[]{:S(2)}, u32[]{:S(2)}) collective-permute-start(bf16[192,1280]{1,0:T(8,128)(2,1)S(1)} %get-tuple-element.35.refs_0_), channel_id=1, source_target_pairs={{0,4},{4,8},{8,12},{12,0},{1,5},{5,9},{9,13},{13,1},{2,6},{6,10},{... | collective-permute-start | bytes 1474568 | tf_op jit(solution)/shard_map/ppermute | solution.py:275
  46.1 1.2 %collective-permute-start.13 = (bf16[320,768]{1,0:T(8,128)(2,1)S(1)}, bf16[320,768]{1,0:T(8,128)(2,1)}, u32[]{:S(2)}, u32[]{:S(2)}) collective-permute-start(bf16[320,768]{1,0:T(8,128)(2,1)S(1)} %get-tuple-element.37.refs_0_), channel_id=1, source_target_pairs={{0,16},{16,32},{32,48},{48,0},{1,17},{17,33},{33,49},{49,1},{2,18}... | collective-permute-start | bytes 1474568 | tf_op jit(solution)/shard_map/ppermute | solution.py:275
  47.4 2.7 %collective-permute-start.10 = (bf16[192,1280]{1,0:T(8,128)(2,1)S(1)}, bf16[192,1280]{1,0:T(8,128)(2,1)S(1)}, u32[]{:S(2)}, u32[]{:S(2)}) collective-permute-start(bf16[192,1280]{1,0:T(8,128)(2,1)S(1)} %get-tuple-element.35.refs_0_), channel_id=1, source_target_pairs={{0,12},{4,0},{8,4},{12,8},{1,13},{5,1},{9,5},{13,9},{2,14},{6,2},{... | collective-permute-start | bytes 1474568 | tf_op jit(solution)/shard_map/ppermute | solution.py:275
  50.0 6.4 %collective-permute-done.11.refs_0_ = bf16[320,768]{1,0:T(8,128)(2,1)S(1)} collective-permute-done((bf16[320,768]{1,0:T(8,128)(2,1)S(1)}, bf16[320,768]{1,0:T(8,128)(2,1)S(1)}, u32[]{:S(2)}, u32[]{:S(2)}) %collective-permute-start.11) | collective-permute-done | bytes 491552 | tf_op jit(solution)/shard_map/ppermute | solution.py:275
  56.4 0.7 collective-permute-start.12
  58.0 0.7 copy.27
  58.6 0.7 broadcast_in_dim_reshape_squeeze.8
  59.3 0.8 %shard_map.167.refs_1_ = bf16[1280,768]{1,0:T(8,128)(2,1)} custom-call(bf16[320,768]{1,0:T(8,128)(2,1)S(1)} %get-tuple-element.37.refs_0_), custom_call_target="tpu_custom_call" | custom-call | tf_op jit(solution)/shard_map/pallas_call | solution.py:249
  60.1 0.8 %shard_map.163.refs_1_ = bf16[768,1280]{1,0:T(8,128)(2,1)} custom-call(bf16[192,1280]{1,0:T(8,128)(2,1)S(1)} %get-tuple-element.35.refs_0_), custom_call_target="tpu_custom_call" | custom-call | tf_op jit(solution)/shard_map/pallas_call | solution.py:249
  60.9 1.8 %shard_map.168.refs_1_ = bf16[1280,768]{1,0:T(8,128)(2,1)} custom-call(bf16[320,768]{1,0:T(8,128)(2,1)} %collective-permute-done.13.refs_0_, bf16[1280,768]{1,0:T(8,128)(2,1)} %shard_map.167.refs_1_), custom_call_target="tpu_custom_call", output_to_operand_aliasing={{}: (1, {})} | custom-call | tf_op jit(solution)/shard_map/pallas_call | solution.py:249
  62.8 0.8 %shard_map.169.refs_1_ = bf16[1280,768]{1,0:T(8,128)(2,1)} custom-call(bf16[320,768]{1,0:T(8,128)(2,1)S(1)} %collective-permute-done.11.refs_0_, bf16[1280,768]{1,0:T(8,128)(2,1)} %shard_map.168.refs_1_), custom_call_target="tpu_custom_call", output_to_operand_aliasing={{}: (1, {})} | custom-call | tf_op jit(solution)/shard_map/pallas_call | solution.py:249
  63.6 0.8 %shard_map.164.refs_1_ = bf16[768,1280]{1,0:T(8,128)(2,1)} custom-call(bf16[192,1280]{1,0:T(8,128)(2,1)S(1)} %collective-permute-done.8.refs_0_, bf16[768,1280]{1,0:T(8,128)(2,1)} %shard_map.163.refs_1_), custom_call_target="tpu_custom_call", output_to_operand_aliasing={{}: (1, {})} | custom-call | tf_op jit(solution)/shard_map/pallas_call | solution.py:249
  64.4 0.8 %shard_map.165.refs_1_ = bf16[768,1280]{1,0:T(8,128)(2,1)} custom-call(bf16[192,1280]{1,0:T(8,128)(2,1)S(1)} %collective-permute-done.10.refs_0_, bf16[768,1280]{1,0:T(8,128)(2,1)} %shard_map.164.refs_1_), custom_call_target="tpu_custom_call", output_to_operand_aliasing={{}: (1, {})} | custom-call | tf_op jit(solution)/shard_map/pallas_call | solution.py:249
  65.2 0.8 %shard_map.170 = bf16[1280,768]{1,0:T(8,128)(2,1)} custom-call(bf16[320,768]{1,0:T(8,128)(2,1)S(1)} %collective-permute-done.12.refs_0_, bf16[1280,768]{1,0:T(8,128)(2,1)} %shard_map.169.refs_1_), custom_call_target="tpu_custom_call", output_to_operand_aliasing={{}: (1, {})} | custom-call | tf_op jit(solution)/shard_map/pallas_call | solution.py:249
  66.1 1.2 %collective-permute-done.9.refs_0_ = bf16[192,1280]{1,0:T(8,128)(2,1)S(1)} collective-permute-done((bf16[192,1280]{1,0:T(8,128)(2,1)S(1)}, bf16[192,1280]{1,0:T(8,128)(2,1)S(1)}, u32[]{:S(2)}, u32[]{:S(2)}) %collective-permute-start.9) | collective-permute-done | bytes 491552 | tf_op jit(solution)/shard_map/ppermute | solution.py:275
  67.3 0.8 %shard_map.166 = bf16[768,1280]{1,0:T(8,128)(2,1)} custom-call(bf16[192,1280]{1,0:T(8,128)(2,1)S(1)} %collective-permute-done.9.refs_0_, bf16[768,1280]{1,0:T(8,128)(2,1)} %shard_map.165.refs_1_), custom_call_target="tpu_custom_call", output_to_operand_aliasing={{}: (1, {})} | custom-call | tf_op jit(solution)/shard_map/pallas_call | solution.py:249
  (16 shorter events, 2.5 us)
Async XLA Ops:
  3.3 12.1 %all-to-all-start = ((f32[8,64,128]{2,1,0:T(8,128)}), f32[8,64,128]{2,1,0:T(8,128)S(1)}, u32[]{:S(2)}, u32[]{:S(2)}) async-start(f32[8,64,128]{2,1,0:T(8,128)} %get-tuple-element.30), calls=%async_computation | async-start | bytes 524288 | tf_op jit(solution)/shard_map/all_to_all | solution.py:294
  7.9 16.6 %collective-permute-start = (f32[24,1280]{1,0:T(8,128)}, f32[24,1280]{1,0:T(8,128)S(1)}, u32[]{:S(2)}, u32[]{:S(2)}) collective-permute-start(f32[24,1280]{1,0:T(8,128)} %get-tuple-element.48), channel_id=1, source_target_pairs={{0,0},{1,64},{2,32},{3,96},{4,4},{5,68},{6,36},{7,100},{8,8},{9,72... | collective-permute-start | bytes 368648 | tf_op jit(solution)/shard_map/ppermute | solution.py:292
  9.4 15.0 %collective-permute-start.1 = (f32[24,1280]{1,0:T(8,128)}, f32[24,1280]{1,0:T(8,128)S(1)}, u32[]{:S(2)}, u32[]{:S(2)}) collective-permute-start(f32[24,1280]{1,0:T(8,128)} %get-tuple-element.48), channel_id=1, source_target_pairs={{0,64},{1,0},{2,96},{3,32},{4,68},{5,4},{6,100},{7,36},{8,72},{9,8... | collective-permute-start | bytes 368648 | tf_op jit(solution)/shard_map/ppermute | solution.py:293
  16.2 15.8 %all-to-all-start.1 = ((f32[16,2,128]{2,1,0:T(2,128)}), f32[16,2,128]{2,1,0:T(2,128)S(1)}, u32[]{:S(2)}, u32[]{:S(2)}) async-start(f32[16,2,128]{2,1,0:T(2,128)} %get-tuple-element.32), calls=%async_computation.1 | async-start | bytes 32768 | tf_op jit(solution)/shard_map/all_to_all | solution.py:296
  32.2 7.5 %collective-permute-start.2 = (bf16[48,1280]{1,0:T(8,128)(2,1)S(1)}, bf16[48,1280]{1,0:T(8,128)(2,1)S(1)}, u32[]{:S(2)}, u32[]{:S(2)}) collective-permute-start(bf16[48,1280]{1,0:T(8,128)(2,1)S(1)} %get-tuple-element.33.g0), channel_id=1, source_target_pairs={{0,16},{16,32},{32,48},{48,0},{1,17},{17,33},{33,49},{49,1},{2,18}... | collective-permute-start | bytes 368648 | tf_op jit(solution)/shard_map/ppermute | solution.py:275
  32.8 8.0 %collective-permute-start.3 = (bf16[48,1280]{1,0:T(8,128)(2,1)S(1)}, bf16[48,1280]{1,0:T(8,128)(2,1)S(1)}, u32[]{:S(2)}, u32[]{:S(2)}) collective-permute-start(bf16[48,1280]{1,0:T(8,128)(2,1)S(1)} %get-tuple-element.33.g0), channel_id=1, source_target_pairs={{0,32},{16,48},{32,0},{48,16},{1,33},{17,49},{33,1},{49,17},{2,34}... | collective-permute-start | bytes 368648 | tf_op jit(solution)/shard_map/ppermute | solution.py:275
  34.9 6.0 %collective-permute-start.4 = (bf16[48,1280]{1,0:T(8,128)(2,1)S(1)}, bf16[48,1280]{1,0:T(8,128)(2,1)S(1)}, u32[]{:S(2)}, u32[]{:S(2)}) collective-permute-start(bf16[48,1280]{1,0:T(8,128)(2,1)S(1)} %get-tuple-element.33.g0), channel_id=1, source_target_pairs={{0,48},{16,0},{32,16},{48,32},{1,49},{17,1},{33,17},{49,33},{2,50}... | collective-permute-start | bytes 368648 | tf_op jit(solution)/shard_map/ppermute | solution.py:275
  36.1 7.4 %collective-permute-start.5 = (bf16[80,768]{1,0:T(8,128)(2,1)S(1)}, bf16[80,768]{1,0:T(8,128)(2,1)S(1)}, u32[]{:S(2)}, u32[]{:S(2)}) collective-permute-start(bf16[80,768]{1,0:T(8,128)(2,1)S(1)} %get-tuple-element.34.d0), channel_id=1, source_target_pairs={{0,4},{4,8},{8,12},{12,0},{1,5},{5,9},{9,13},{13,1},{2,6},{6,10},{... | collective-permute-start | bytes 368648 | tf_op jit(solution)/shard_map/ppermute | solution.py:275
  36.6 6.8 %collective-permute-start.6 = (bf16[80,768]{1,0:T(8,128)(2,1)S(1)}, bf16[80,768]{1,0:T(8,128)(2,1)S(1)}, u32[]{:S(2)}, u32[]{:S(2)}) collective-permute-start(bf16[80,768]{1,0:T(8,128)(2,1)S(1)} %get-tuple-element.34.d0), channel_id=1, source_target_pairs={{0,8},{4,12},{8,0},{12,4},{1,9},{5,13},{9,1},{13,5},{2,10},{6,14},... | collective-permute-start | bytes 368648 | tf_op jit(solution)/shard_map/ppermute | solution.py:275
  39.7 4.9 %collective-permute-start.7 = (bf16[80,768]{1,0:T(8,128)(2,1)S(1)}, bf16[80,768]{1,0:T(8,128)(2,1)S(1)}, u32[]{:S(2)}, u32[]{:S(2)}) collective-permute-start(bf16[80,768]{1,0:T(8,128)(2,1)S(1)} %get-tuple-element.34.d0), channel_id=1, source_target_pairs={{0,12},{4,0},{8,4},{12,8},{1,13},{5,1},{9,5},{13,9},{2,14},{6,2},{... | collective-permute-start | bytes 368648 | tf_op jit(solution)/shard_map/ppermute | solution.py:275
  44.7 11.7 %collective-permute-start.11 = (bf16[320,768]{1,0:T(8,128)(2,1)S(1)}, bf16[320,768]{1,0:T(8,128)(2,1)S(1)}, u32[]{:S(2)}, u32[]{:S(2)}) collective-permute-start(bf16[320,768]{1,0:T(8,128)(2,1)S(1)} %get-tuple-element.37.refs_0_), channel_id=1, source_target_pairs={{0,48},{16,0},{32,16},{48,32},{1,49},{17,1},{33,17},{49,33},{2,50}... | collective-permute-start | bytes 1474568 | tf_op jit(solution)/shard_map/ppermute | solution.py:275
  45.4 11.8 %collective-permute-start.8 = (bf16[192,1280]{1,0:T(8,128)(2,1)S(1)}, bf16[192,1280]{1,0:T(8,128)(2,1)S(1)}, u32[]{:S(2)}, u32[]{:S(2)}) collective-permute-start(bf16[192,1280]{1,0:T(8,128)(2,1)S(1)} %get-tuple-element.35.refs_0_), channel_id=1, source_target_pairs={{0,4},{4,8},{8,12},{12,0},{1,5},{5,9},{9,13},{13,1},{2,6},{6,10},{... | collective-permute-start | bytes 1474568 | tf_op jit(solution)/shard_map/ppermute | solution.py:275
  46.1 14.8 %collective-permute-start.13 = (bf16[320,768]{1,0:T(8,128)(2,1)S(1)}, bf16[320,768]{1,0:T(8,128)(2,1)}, u32[]{:S(2)}, u32[]{:S(2)}) collective-permute-start(bf16[320,768]{1,0:T(8,128)(2,1)S(1)} %get-tuple-element.37.refs_0_), channel_id=1, source_target_pairs={{0,16},{16,32},{32,48},{48,0},{1,17},{17,33},{33,49},{49,1},{2,18}... | collective-permute-start | bytes 1474568 | tf_op jit(solution)/shard_map/ppermute | solution.py:275
  47.4 17.0 %collective-permute-start.10 = (bf16[192,1280]{1,0:T(8,128)(2,1)S(1)}, bf16[192,1280]{1,0:T(8,128)(2,1)S(1)}, u32[]{:S(2)}, u32[]{:S(2)}) collective-permute-start(bf16[192,1280]{1,0:T(8,128)(2,1)S(1)} %get-tuple-element.35.refs_0_), channel_id=1, source_target_pairs={{0,12},{4,0},{8,4},{12,8},{1,13},{5,1},{9,5},{13,9},{2,14},{6,2},{... | collective-permute-start | bytes 1474568 | tf_op jit(solution)/shard_map/ppermute | solution.py:275
  56.4 8.8 %collective-permute-start.12 = (bf16[320,768]{1,0:T(8,128)(2,1)S(1)}, bf16[320,768]{1,0:T(8,128)(2,1)S(1)}, u32[]{:S(2)}, u32[]{:S(2)}) collective-permute-start(bf16[320,768]{1,0:T(8,128)(2,1)S(1)} %collective-permute-done.11.refs_0_), channel_id=1, source_target_pairs={{0,48},{16,0},{32,16},{48,32},{1,49},{17,1},{33,17},{49,33},{2,50}... | collective-permute-start | bytes 1474568 | tf_op jit(solution)/shard_map/ppermute | solution.py:275
  57.3 10.0 %collective-permute-start.9 = (bf16[192,1280]{1,0:T(8,128)(2,1)S(1)}, bf16[192,1280]{1,0:T(8,128)(2,1)S(1)}, u32[]{:S(2)}, u32[]{:S(2)}) collective-permute-start(bf16[192,1280]{1,0:T(8,128)(2,1)S(1)} %collective-permute-done.8.refs_0_), channel_id=1, source_target_pairs={{0,4},{4,8},{8,12},{12,0},{1,5},{5,9},{9,13},{13,1},{2,6},{6,10},{... | collective-permute-start | bytes 1474568 | tf_op jit(solution)/shard_map/ppermute | solution.py:275
